TPU v7x, 256 devices: a whole 4x4x8 slice. The times are simulated.
256 devices in a mesh: dp: 256 (over y, x, z, core).
Axes of the slice: x: 4, y: 4, z: 8, core: 2. Of those that a mesh axis runs over, the one named last changes fastest.
Arguments:
- inputs: bfloat16 [65536, 4096], P('dp'), may hold values from -6 to 6
- out_grads: bfloat16 [65536, 512], P('dp'), may hold values from -6 to 6
- feedback: bfloat16 [1048576, 512], P('dp'), may hold values from -4 to 4
- q_start: float32 [512, 64], replicated, may hold values from -6 to 6
Outputs:
- update: float32 [4096, 512], P('dp')
- q_next: float32 [512, 64], replicated
- new_feedback: bfloat16 [1048576, 512], P('dp')
All inputs are finite; a program needn't handle non-finite values.
Results may differ from a plain program's by a relative error of at most 0.001.
Values sent between devices are 32-bit elements; how exact they have to be, the bound alone decides.
A program may use at most 64 MiB of HBM per device.

v0:
```python
import jax
import jax.numpy as jnp
from jax import lax
from jax.sharding import PartitionSpec as P

HIGH = lax.Precision.HIGHEST


def body(inputs, out_grads, feedback, q_start):
    tok_rows = inputs.shape[0]
    replicas = lax.axis_size("dp")
    grad = lax.dot_general(
        inputs, out_grads, (((0,), (0,)), ((), ())), preferred_element_type=jnp.float32
    )
    matrix = grad * (1.0 / jnp.sqrt(jnp.float32(tok_rows))) + feedback.astype(jnp.float32)
    p_block = lax.psum_scatter(
        jnp.dot(matrix, q_start, precision=HIGH), "dp", scatter_dimension=0, tiled=True
    )
    gram = lax.psum(jnp.dot(p_block.T, p_block, precision=HIGH), "dp")
    lower = jnp.linalg.cholesky(gram)
    orth_block = jax.scipy.linalg.solve_triangular(lower, p_block.T, lower=True).T
    p_orth = lax.all_gather(orth_block, "dp", axis=0, tiled=True)
    q_part = lax.dot_general(
        matrix, p_orth, (((0,), (0,)), ((), ())), precision=HIGH, preferred_element_type=jnp.float32
    )
    q_next = lax.psum(q_part, "dp") / jnp.float32(replicas)
    update = jnp.dot(orth_block, q_next.T, precision=HIGH)
    new_feedback = (matrix - jnp.dot(p_orth, q_next.T, precision=HIGH)).astype(jnp.bfloat16)
    return (update, q_next, new_feedback)


def solution(mesh):
    placed = (P("dp", None), P("dp", None), P("dp", None), P())
    return jax.shard_map(
        body,
        mesh=mesh,
        in_specs=placed,
        out_specs=(P("dp", None), P(), P("dp", None)),
        check_vma=False,
    )
```

profile of v0, /device:TPU:1, one launch (start us, length us, event | category | flops | bytes accessed | tf_op | source)
XLA Modules:
  0.0 1751.4 jit_solution(2437911735306431260)
XLA Ops:
  7.2 0.0 copy-start
  7.2 0.0 copy-start.3
  7.2 0.0 reduce-scatter.2.cloned.1.call-start
  7.2 1.5 copy-done
  8.8 3.6 convert_add_fusion
  12.3 0.0 copy-start.1
  12.3 3.2 copy-done.1
  15.6 0.0 copy-done.3
  15.6 8.1 fusion.4
  23.6 0.0 reduce-scatter.2.cloned.1.call-update
  23.6 0.0 all-gather.2.cloned.1.call-start
  23.7 1266.8 %reduce-scatter.2.cloned.1.call-done = f32[16,64]{1,0:T(8,128)} async-done(((f32[4096,64]{1,0:T(8,128)}), f32[16,64]{1,0:T(8,128)}) %reduce-scatter.2.cloned.1.call-update) | async-done | bytes 4112 | tf_op jit(solution)/shard_map/reduce_scatter | solution.py:16
  1290.5 1.0 fusion.5
  1291.5 78.3 %psum.14 = f32[64,64]{0,1:T(8,128)S(1)} all-reduce(f32[64,64]{0,1:T(8,128)S(1)} %fusion.5), channel_id=1, replica_groups=mesh['dp'=256] {'dp'}, use_global_device_ids=true, to_apply=%region_1.0 | all-reduce | flops 4096 | bytes 32768 | tf_op jit(solution)/shard_map/psum | solution.py:19
  1369.9 0.1 copy.8
  1369.9 5.8 cholesky.16
  1375.8 0.6 compare_reduce_fusion
  1376.5 0.7 fusion
  1377.1 4.9 custom-call.7
  1382.0 1.5 fusion.1
  1383.5 0.0 all-gather.2.cloned.1.call-update
  1383.5 0.0 copy-start.4
  1383.5 0.2 all-reduce.2.cloned.1.call-start
  1383.8 99.7 %all-gather.2.cloned.1.call-done = f32[4096,64]{1,0:T(8,128)} async-done(((f32[16,64]{1,0:T(8,128)}), f32[4096,64]{1,0:T(8,128)}) %all-gather.2.cloned.1.call-update) | async-done | bytes 1048592 | tf_op jit(solution)/shard_map/all_gather | solution.py:22
  1483.4 9.3 fusion.6
  1492.7 0.0 all-reduce.2.cloned.1.call-update
  1492.7 239.4 %all-reduce.2.cloned.1.call-done = f32[512,64]{0,1:T(8,128)} async-done(((f32[512,64]{0,1:T(8,128)}), f32[512,64]{0,1:T(8,128)}) %all-reduce.2.cloned.1.call-update) | async-done | bytes 131088 | tf_op jit(solution)/shard_map/psum | solution.py:26
  1732.1 0.9 broadcast_multiply_fusion
  1733.0 0.0 copy-done.4
  1733.0 0.0 copy-start.2
  1733.0 0.8 fusion.7
  1733.8 11.0 subtract_convert_fusion
  1744.9 0.0 copy-done.2
  (2 shorter events, 0.0 us)
Async XLA Ops:
  7.2 1.6 copy-start
  7.2 8.4 copy-start.3
  7.2 1283.3 %reduce-scatter.2.cloned.1.call-start = ((), (), s32[]{:S(2)}) async-start(), calls=%async_computation.1 | async-start | bytes 2105344 | tf_op jit(solution)/shard_map/reduce_scatter | solution.py:16
  12.3 3.2 copy-start.1
  23.6 1459.8 %all-gather.2.cloned.1.call-start = ((), (), s32[]{:S(2)}) async-start(), calls=%async_computation.2 | async-start | bytes 2105344 | tf_op jit(solution)/shard_map/all_gather | solution.py:22
  1383.5 349.5 %copy-start.4 = (f32[64,16]{0,1:T(8,128)S(1)}, f32[64,16]{0,1:T(8,128)}, u32[]{:S(2)}) copy-start(f32[64,16]{0,1:T(8,128)} %fusion.1) | copy-start | bytes 12292
  1383.5 348.6 %all-reduce.2.cloned.1.call-start = ((), (), s32[]{:S(2)}) async-start(), calls=%async_computation.3 | async-start | bytes 262144 | tf_op jit(solution)/shard_map/psum | solution.py:26
  1733.0 11.8 copy-start.2
Sparse Core Ops, SparseCore 0:
  23.8 1266.6 reduce-scatter.1
  1383.6 99.7 all-gather.1
  1492.8 239.2 all-reduce.1
where the time goes:
time: 1750 us
  waiting for transfers between devices  1610 us (92%)
  blocking collectives  78.3 us (4%)
  matrix products  35.2 us (2%)
    reduce_scatter x1, waiting for transfers between devices, body(): lax.psum_scatter(jnp.dot(matrix, q_start, precision=HIGH), 'dp', scatter_...  1270 us
    psum x1, waiting for transfers between devices, body(): q_next = lax.psum(q_part, 'dp') / jnp.float32(replicas)  239 us
    all_gather x1, waiting for transfers between devices, body(): p_orth = lax.all_gather(orth_block, 'dp', axis=0, tiled=True)  99.7 us
    psum x1, blocking collectives, body(): gram = lax.psum(jnp.dot(p_block.T, p_block, precision=HIGH), 'dp')  78.3 us
  transfers between devices with their start and end apart: 3, of which 3 were waited for; matrix products, arithmetic and copies ran while one was open for 0% of the time, Pallas kernels for 0%

commit v1 on v0

v1 whole, which is shorter than its diff:
```python
import jax
import jax.numpy as jnp
from jax import lax
from jax.experimental import pallas as pl
from jax.experimental.pallas import tpu as pltpu
from jax.sharding import PartitionSpec as P

HIGH = lax.Precision.HIGHEST
MESH = pl.DeviceIdType.MESH
F32, BF16 = jnp.float32, jnp.bfloat16

D, KV, RANK, TOK, N_DP = 4096, 512, 64, 256, 256
CH = 512
PLANE = [(dy, dx) for dy in range(4) for dx in range(4) if (dy, dx) != (0, 0)]


def nn(a, b):
    return lax.dot_general(a, b, (((1,), (0,)), ((), ())), preferred_element_type=F32)


def nt(a, b):
    return lax.dot_general(a, b, (((1,), (1,)), ((), ())), preferred_element_type=F32)


def tn(a, b):
    return lax.dot_general(a, b, (((0,), (0,)), ((), ())), preferred_element_type=F32)


def split(v, pieces):
    out = []
    for at in range(pieces):
        out.append(v.astype(BF16))
        if at < pieces - 1:
            v = v - out[-1].astype(F32)
    return out


def fold(t):
    return (t[128:192] + t[64:128]) + t[0:64]


def eliminate(a, first, last):
    rows = lax.broadcasted_iota(jnp.int32, (RANK, 1), 0)
    for k in range(first, last):
        row = a[k : k + 1, :]
        ratio = a[:, k : k + 1] / a[k : k + 1, k : k + 1]
        a = a - jnp.where(rows > k, ratio, 0.0) * row
    return a


def kernel(
    x_hbm, g_hbm, f_hbm, q_hbm, upd_ref, qn_ref, out_hbm,
    x_v, g_v, f_v, q_v, m_v, out_v, pt_v, p_full,
    core_send, core_recv, acc, plane_recv, z_send, z_recv,
    gram_v, st_v, y_v, s_send, s_recv, s_part, s_group, s_full,
    load_sem, x_sem, f_sem, out_sem,
    core_ss, core_rs, plane_ss, plane_rs, z_ss, z_rs,
    zg_ss, zg_rs, pg_ss, pg_rs, cg_ss, cg_rs,
    s1_ss, s1_rs, s2_ss, s2_rs, s3_ss, s3_rs,
):
    me = lax.axis_index("dp")
    core = lax.rem(me, 2)
    z = lax.rem(lax.div(me, 2), 8)
    group = lax.rem(me, 16)
    plane = lax.div(me, 16)
    y, x = lax.div(plane, 4), lax.rem(plane, 4)
    partner = me + 1 - 2 * core
    block = core * 16 + plane

    def plane_peer(dy, dx):
        return (lax.rem(y + dy, 4) * 4 + lax.rem(x + dx, 4)) * 16 + group

    def z_peer(dz):
        return plane * 16 + lax.rem(z + dz, 8) * 2 + core

    def group_peer(d):
        return plane * 16 + lax.rem(group + d, 16)

    def send(src, dst, ss, rs, device):
        copy = pltpu.make_async_remote_copy(
            src_ref=src, dst_ref=dst, send_sem=ss, recv_sem=rs,
            device_id=(device,), device_id_type=MESH,
        )
        copy.start()
        return copy

    started = []

    order = [lax.rem(y + t + 1, 4) for t in range(4)]
    chunks = [(1 - core) * 4 + c for c in order] + [core * 4 + c for c in order]
    loads = [
        pltpu.make_async_copy(q_hbm, q_v, load_sem.at[0]),
        pltpu.make_async_copy(g_hbm, g_v, load_sem.at[1]),
    ]
    for copy in loads:
        copy.start()
    x_loads, f_loads = [], []
    for i, c in enumerate(chunks):
        at = pl.ds(pl.multiple_of(c * CH, CH), CH)
        f_loads.append(pltpu.make_async_copy(f_hbm.at[at, :], f_v.at[at, :], f_sem.at[i]))
        x_loads.append(pltpu.make_async_copy(x_hbm.at[:, at], x_v.at[:, at], x_sem.at[i]))
        f_loads[-1].start()
        x_loads[-1].start()

    barrier = pltpu.get_barrier_semaphore()
    for dy, dx in PLANE:
        pl.semaphore_signal(barrier, inc=1, device_id=(plane_peer(dy, dx),), device_id_type=MESH)
    for d in range(1, 16):
        pl.semaphore_signal(barrier, inc=1, device_id=(group_peer(d),), device_id_type=MESH)

    for copy in loads:
        copy.wait()
    q3 = jnp.concatenate(split(q_v[...].T, 3), axis=0)
    gq3 = jnp.concatenate(split(fold(nt(q3, g_v[...])) * (1.0 / 16.0), 3), axis=0)

    def part(i):
        f_loads[i].wait()
        x_loads[i].wait()
        at = pl.ds(pl.multiple_of(chunks[i] * CH, CH), CH)
        return fold(nt(q3, f_v[at, :]) + nn(gq3, x_v[:, at]))

    core_copies = []
    for t in range(4):
        v = part(t)
        for i in range(4):
            core_send[t * 4 + i] = v[:, i * 128 : (i + 1) * 128]
        if t == 0:
            pl.semaphore_wait(barrier, 30)
        at = pl.ds(t * 4, 4)
        core_copies.append(send(core_send.at[at], core_recv.at[at], core_ss.at[t], core_rs.at[t], partner))
    plane_copies = {}
    for t in range(4):
        v = part(4 + t)
        core_copies[t].wait_recv()
        for i in range(4):
            acc[t * 4 + i] = v[:, i * 128 : (i + 1) * 128] + core_recv[t * 4 + i]
        dy = (t + 1) % 4
        for dx in range(4):
            d = dy * 4 + dx
            if d == 0:
                continue
            plane_copies[d] = send(
                acc.at[t * 4 + lax.rem(x + dx, 4)], plane_recv.at[d],
                plane_ss.at[d], plane_rs.at[d], plane_peer(dy, dx),
            )
    started += core_copies + list(plane_copies.values())

    def matrix(i, carry):
        at = pl.ds(pl.multiple_of(i * 256, 256), 256)
        m_v[at, :] = tn(x_v[:, at], g_v[...]) * (1.0 / 16.0) + f_v[at, :].astype(F32)
        return carry

    lax.fori_loop(0, D // 256, matrix, 0)

    s = acc[12 + x]
    for d in range(1, 16):
        plane_copies[d].wait_recv()
        s = s + plane_recv[d]
    for k in range(8):
        z_send[k] = s[k * 8 : (k + 1) * 8]
    z_copies = {}
    for dz in range(1, 8):
        z_copies[dz] = send(
            z_send.at[lax.rem(z + dz, 8)], z_recv.at[dz], z_ss.at[dz], z_rs.at[dz], z_peer(dz)
        )
    s = z_send[z]
    for dz in range(1, 8):
        z_copies[dz].wait_recv()
        s = s + z_recv[dz]
    p_full[block, z] = s
    started += list(z_copies.values())

    own = p_full.at[block, z]
    z_gathers = [send(own, own, zg_ss.at[dz], zg_rs.at[dz], z_peer(dz)) for dz in range(1, 8)]
    for copy in z_gathers:
        copy.wait_recv()
    mine = p_full.at[block]
    plane_gathers = {}
    for dy, dx in PLANE:
        d = dy * 4 + dx
        plane_gathers[d] = send(mine, mine, pg_ss.at[d], pg_rs.at[d], plane_peer(dy, dx))
    started += z_gathers + list(plane_gathers.values())

    def consume(c, first):
        p = p_full[pl.ds(c * 4, 4)].reshape(4, RANK, 128)
        p = jnp.concatenate([p[i] for i in range(4)], axis=1)
        p1, p2, p3 = split(p, 3)
        p3 = jnp.concatenate([p1, p2, p3], axis=0)
        at = pl.ds(pl.multiple_of(c * CH, CH), CH)
        gram, yt, st = nt(p3, p3), nt(p3, x_v[:, at]), nn(p3, f_v[at, :])
        gram_v[...] = gram if first else gram_v[...] + gram
        y_v[...] = yt if first else y_v[...] + yt
        st_v[...] = st if first else st_v[...] + st
        pt_v[at, :] = p3[0:128].T

    core_gathers = []
    for dy in range(4):
        for dx in range(4):
            if dy * 4 + dx > 0:
                plane_gathers[dy * 4 + dx].wait_recv()
        c = core * 4 + lax.rem(y + 4 - dy, 4)
        rows = p_full.at[pl.ds(c * 4, 4)]
        core_gathers.append(send(rows, rows, cg_ss.at[dy], cg_rs.at[dy], partner))
        consume(c, dy == 0)
    for dy in range(4):
        core_gathers[dy].wait_recv()
        consume((1 - core) * 4 + lax.rem(y + 4 - dy, 4), False)
    started += core_gathers

    y3 = jnp.concatenate(split(fold(y_v[...]) * (1.0 / 16.0), 3), axis=0)
    s = fold(st_v[...] + nn(y3, g_v[...]))
    for p in range(16):
        s_send[p] = s[(p // 2) * 8 : (p // 2) * 8 + 8, (p % 2) * 256 : (p % 2) * 256 + 256]
    s1 = {}
    for dy, dx in PLANE:
        d = dy * 4 + dx
        to = lax.rem(y + dy, 4) * 4 + lax.rem(x + dx, 4)
        s1[d] = send(s_send.at[to], s_recv.at[d], s1_ss.at[d], s1_rs.at[d], plane_peer(dy, dx))

    gram = gram_v[...]
    gram = fold(gram)
    gram = (gram[:, 128:192] + gram[:, 64:128]) + gram[:, 0:64]
    rows = lax.broadcasted_iota(jnp.int32, (RANK, RANK), 0)
    cols = lax.broadcasted_iota(jnp.int32, (RANK, RANK), 1)
    eye = (rows == cols).astype(F32)
    a = jnp.concatenate([gram, eye], axis=1)
    a = eliminate(a, 0, 22)

    s = s_send[plane]
    for d in range(1, 16):
        s1[d].wait_recv()
        s = s + s_recv[d]
    s_part[...] = s
    s_group[group] = s
    s2 = []
    for d in range(1, 16):
        s2.append(send(s_part, s_group.at[group], s2_ss.at[d], s2_rs.at[d], group_peer(d)))
    a = eliminate(a, 22, 43)
    for copy in s2:
        copy.wait_recv()
    s = s_group[0]
    for k in range(1, 16):
        s = s + s_group[k]
    s_full[plane] = s
    s3 = []
    for dy, dx in PLANE:
        d = dy * 4 + dx
        s3.append(send(s_full.at[plane], s_full.at[plane], s3_ss.at[d], s3_rs.at[d], plane_peer(dy, dx)))
    a = eliminate(a, 43, 64)
    diag = jnp.sum(a[:, 0:64] * eye, axis=1, keepdims=True)
    inv = a[:, 64:128] * (1.0 / jnp.sqrt(diag))
    inv_t = inv.T
    for copy in s3:
        copy.wait_recv()
    started += list(s1.values()) + s2 + s3

    s = jnp.concatenate(
        [jnp.concatenate([s_full[2 * r], s_full[2 * r + 1]], axis=1) for r in range(8)], axis=0
    )
    qn = jnp.dot(inv, s, precision=HIGH, preferred_element_type=F32) * (1.0 / N_DP)
    w = jnp.dot(inv_t, qn, precision=HIGH, preferred_element_type=F32)
    w1, w2 = split(w, 2)
    w = jnp.concatenate([w1, w1, w2, w2], axis=0)

    def finish(i, carry):
        at = pl.ds(pl.multiple_of(i * 256, 256), 256)
        p = pt_v[at, :]
        o = m_v[at, :] - nn(jnp.concatenate([p, p], axis=1), w)
        out_v[at, :] = o.astype(BF16)
        pltpu.make_async_copy(out_v.at[at, :], out_hbm.at[at, :], out_sem.at[i]).start()
        return carry

    lax.fori_loop(0, D // 256, finish, 0)
    p = pt_v[pl.ds(pl.multiple_of(me * 16, 16), 16), :]
    upd_ref[...] = nn(jnp.concatenate([p, p], axis=1), w)
    qn_ref[...] = qn.T
    for copy in started:
        copy.wait_send()

    def landed(i, carry):
        at = pl.ds(pl.multiple_of(i * 256, 256), 256)
        pltpu.make_async_copy(out_v.at[at, :], out_hbm.at[at, :], out_sem.at[i]).wait()
        return carry

    lax.fori_loop(0, D // 256, landed, 0)


def body(inputs, out_grads, feedback, q_start):
    dma = pltpu.SemaphoreType.DMA
    vmem = pltpu.VMEM
    return pl.pallas_call(
        kernel,
        out_shape=(
            jax.ShapeDtypeStruct((D // N_DP, KV), F32),
            jax.ShapeDtypeStruct((KV, RANK), F32),
            jax.ShapeDtypeStruct((D, KV), BF16),
        ),
        in_specs=[pl.BlockSpec(memory_space=pl.ANY)] * 4,
        out_specs=(
            pl.BlockSpec(memory_space=vmem),
            pl.BlockSpec(memory_space=vmem),
            pl.BlockSpec(memory_space=pl.ANY),
        ),
        scratch_shapes=[
            vmem((TOK, D), BF16),
            vmem((TOK, KV), BF16),
            vmem((D, KV), BF16),
            vmem((KV, RANK), F32),
            vmem((D, KV), F32),
            vmem((D, KV), BF16),
            vmem((D, 128), BF16),
            vmem((32, 8, 8, 128), F32),
            vmem((16, RANK, 128), F32),
            vmem((16, RANK, 128), F32),
            vmem((16, RANK, 128), F32),
            vmem((16, RANK, 128), F32),
            vmem((8, 8, 128), F32),
            vmem((8, 8, 128), F32),
            vmem((192, 192), F32),
            vmem((192, KV), F32),
            vmem((192, TOK), F32),
            vmem((16, 8, 256), F32),
            vmem((16, 8, 256), F32),
            vmem((8, 256), F32),
            vmem((16, 8, 256), F32),
            vmem((16, 8, 256), F32),
            dma((2,)), dma((8,)), dma((8,)), dma((16,)),
            dma((4,)), dma((4,)), dma((16,)), dma((16,)), dma((8,)), dma((8,)),
            dma((8,)), dma((8,)), dma((16,)), dma((16,)), dma((4,)), dma((4,)),
            dma((16,)), dma((16,)), dma((16,)), dma((16,)), dma((16,)), dma((16,)),
        ],
        compiler_params=pltpu.CompilerParams(
            collective_id=0, has_side_effects=True, vmem_limit_bytes=48 * 1024 * 1024
        ),
    )(inputs, out_grads, feedback, q_start)


def solution(mesh):
    placed = (P("dp", None), P("dp", None), P("dp", None), P())
    return jax.shard_map(
        body,
        mesh=mesh,
        in_specs=placed,
        out_specs=(P("dp", None), P(), P("dp", None)),
        check_vma=False,
    )
```

time: 1750 us -> 75.4 us (0.04)
  waiting for transfers between devices: 1610 us -> 0 us
  blocking collectives: 78.3 us -> 0 us
  Pallas kernels: 0 us -> 65.2 us
  matrix products: 35.2 us -> 0 us
    reduce_scatter x1 -> x0, waiting for transfers between devices: 1270 us -> none  [body(): lax.psum_scatter(jnp.dot(matrix, q_start, precision=HIGH), 'dp', scatter_...]
    psum x1 -> x0, waiting for transfers between devices: 239 us -> none  [body(): q_next = lax.psum(q_part, 'dp') / jnp.float32(replicas)]
    all_gather x1 -> x0, waiting for transfers between devices: 99.7 us -> none  [body(): p_orth = lax.all_gather(orth_block, 'dp', axis=0, tiled=True)]
    psum x1 -> x0, blocking collectives: 78.3 us -> none  [body(): gram = lax.psum(jnp.dot(p_block.T, p_block, precision=HIGH), 'dp')]
    pallas_call x0 -> x1, Pallas kernels: none -> 65.2 us  [body(): pl.pallas_call(kernel, out_shape=(jax.ShapeDtypeStruct((D // N_DP, KV), F...]
    dot_general x6 -> x0, matrix products: 33.7 us -> none  [the longest x1 11 us: body(): jnp.dot(p_orth, q_next.T, precision=HIGH)]
  transfers between devices with their start and end apart: 3 -> 0, of which waited for: 3 -> 0; matrix products, arithmetic and copies ran while one was open for 0% -> 0% of each run, Pallas kernels for 0% -> 0%
where the time goes in v1:
time: 75.4 us; the launch traced here: 75.2 us
  Pallas kernels  65.2 us (86%)
  local copies, waits for them, and re-layouts  9.42 us (12%)
    pallas_call x1, Pallas kernels, body(): pl.pallas_call(kernel, out_shape=(jax.ShapeDtypeStruct((D // N_DP, KV), F...  65.2 us
    unnamed x7, local copies, waits for them, and re-layouts  8.65 us

profile of v1, /device:TPU:1, one launch (start us, length us, event | category | flops | bytes accessed | tf_op | source)
XLA Modules:
  0.0 75.2 jit_solution(5931758886465781854)
XLA Ops:
  0.6 1.0 %copy.7.q_hbm = f32[512,64]{1,0:T(8,128)S(1)} copy(f32[512,64]{0,1:T(8,128)} %param.7) | data formatting | bytes 262144 | tf_op args[3]
  1.7 0.0 copy-start
  1.7 1.6 %copy-done = bf16[256,4096]{1,0:T(8,128)(2,1)S(1)} copy-done((bf16[256,4096]{1,0:T(8,128)(2,1)S(1)}, bf16[256,4096]{1,0:T(8,128)(2,1)}, u32[]{:S(2)}) %copy-start) | copy-done | bytes 2097176
  3.3 0.0 copy-start.1
  3.3 0.9 %copy-done.1 = bf16[256,512]{1,0:T(8,128)(2,1)S(1)} copy-done((bf16[256,512]{1,0:T(8,128)(2,1)S(1)}, bf16[256,512]{1,0:T(8,128)(2,1)}, u32[]{:S(2)}) %copy-start.1) | copy-done | bytes 262168
  4.2 65.2 %shard_map.67 = (f32[16,512]{1,0:T(8,128)S(1)}, f32[512,64]{1,0:T(8,128)S(1)}, bf16[4096,512]{1,0:T(8,128)(2,1)}) custom-call(bf16[256,4096]{1,0:T(8,128)(2,1)S(1)} %copy-done, bf16[256,512]{1,0:T(8,128)(2,1)S(1)} %copy-done.1, bf16[4096,512]{1,0:T(8,128)(2,1)} %f_hbm.1, f32[512,64]{1,0:T(8,128)S(1)} %copy.7.q_hbm), custom_call_target="tpu_custom_call" | custom-call | tf_op jit(solution)/shard_map/pallas_call | solution.py:291
  69.4 0.8 %copy.8 = f32[512,64]{0,1:T(8,128)} copy(f32[512,64]{1,0:T(8,128)S(1)} %get-tuple-element.4) | data formatting | bytes 262144 | tf_op jit(solution)/shard_map/pallas_call | solution.py:291
  70.2 0.6 copy.11
  70.8 4.5 %copy.12 = bf16[4096,512]{1,0:T(8,128)(2,1)} copy(bf16[4096,512]{1,0:T(8,128)(2,1)} %get-tuple-element.11) | data formatting | bytes 8388608
Async XLA Ops:
  1.7 1.6 %copy-start = (bf16[256,4096]{1,0:T(8,128)(2,1)S(1)}, bf16[256,4096]{1,0:T(8,128)(2,1)}, u32[]{:S(2)}) copy-start(bf16[256,4096]{1,0:T(8,128)(2,1)} %x_hbm.1) | copy-start | bytes 6291460
  3.3 0.9 %copy-start.1 = (bf16[256,512]{1,0:T(8,128)(2,1)S(1)}, bf16[256,512]{1,0:T(8,128)(2,1)}, u32[]{:S(2)}) copy-start(bf16[256,512]{1,0:T(8,128)(2,1)} %g_hbm.1) | copy-start | bytes 786436

commit v2 on v1

v2 whole, which is shorter than its diff:
```python
import jax
import jax.numpy as jnp
from jax import lax
from jax.experimental import pallas as pl
from jax.experimental.pallas import tpu as pltpu
from jax.sharding import PartitionSpec as P

HIGH = lax.Precision.HIGHEST
MESH = pl.DeviceIdType.MESH
F32, BF16 = jnp.float32, jnp.bfloat16

D, KV, RANK, TOK, N_DP = 4096, 512, 64, 256, 256
CH = 512
HALF = RANK // 2
PLANE = [(dy, dx) for dy in range(4) for dx in range(4) if (dy, dx) != (0, 0)]
MIB = 1024 * 1024


def nn(a, b):
    return lax.dot_general(a, b, (((1,), (0,)), ((), ())), preferred_element_type=F32)


def nt(a, b):
    return lax.dot_general(a, b, (((1,), (1,)), ((), ())), preferred_element_type=F32)


def tn(a, b):
    return lax.dot_general(a, b, (((0,), (0,)), ((), ())), preferred_element_type=F32)


def split(v, pieces):
    out = []
    for at in range(pieces):
        out.append(v.astype(BF16))
        if at < pieces - 1:
            v = v - out[-1].astype(F32)
    return out


def fold(t):
    return (t[128:192] + t[64:128]) + t[0:64]


def eliminate(a, first, last):
    rows = lax.broadcasted_iota(jnp.int32, (RANK, 1), 0)
    for k in range(first, last):
        row = a[k : k + 1, :]
        ratio = a[:, k : k + 1] / a[k : k + 1, k : k + 1]
        a = a - jnp.where(rows > k, ratio, 0.0) * row
    return a


def kernel(
    x_hbm, g_hbm, f_hbm, q_hbm, upd_ref, qn_ref, m_ref, pt_ref, w_ref,
    x_v, g_v, f_v, q_v, p_full,
    terms, core_recv, acc, plane_recv, z_group,
    gram_v, st_v, y_v, s_send, s_recv, s_group, s_core, s_full,
    load_sem, x_sem, f_sem,
    core_ss, core_rs, plane_ss, plane_rs, z_ss, z_rs,
    pg_ss, pg_rs, cg_ss, cg_rs,
    s1_ss, s1_rs, s2_ss, s2_rs, sc_ss, sc_rs, s3_ss, s3_rs,
):
    me = lax.axis_index("dp")
    core = lax.rem(me, 2)
    z = lax.rem(lax.div(me, 2), 8)
    group = lax.rem(me, 16)
    plane = lax.div(me, 16)
    y, x = lax.div(plane, 4), lax.rem(plane, 4)
    partner = me + 1 - 2 * core
    own = pl.ds(pl.multiple_of(core * HALF, HALF), HALF)
    other = pl.ds(pl.multiple_of((1 - core) * HALF, HALF), HALF)

    def plane_peer(dy, dx):
        return (lax.rem(y + dy, 4) * 4 + lax.rem(x + dx, 4)) * 16 + group

    def z_peer(dz):
        return plane * 16 + lax.rem(z + dz, 8) * 2 + core

    started = []

    def send(src, dst, ss, rs, device):
        copy = pltpu.make_async_remote_copy(
            src_ref=src, dst_ref=dst, send_sem=ss, recv_sem=rs,
            device_id=(device,), device_id_type=MESH,
        )
        copy.start()
        started.append(copy)
        return copy

    order = [lax.rem(y + t + 1, 4) for t in range(4)]
    chunks = order + [4 + c for c in order]
    loads = [
        pltpu.make_async_copy(q_hbm, q_v, load_sem.at[0]),
        pltpu.make_async_copy(g_hbm, g_v, load_sem.at[1]),
    ]
    for copy in loads:
        copy.start()
    x_loads, f_loads = [], []
    for i, c in enumerate(chunks):
        at = pl.ds(pl.multiple_of(c * CH, CH), CH)
        f_loads.append(pltpu.make_async_copy(f_hbm.at[at, :], f_v.at[at, :], f_sem.at[i]))
        x_loads.append(pltpu.make_async_copy(x_hbm.at[:, at], x_v.at[:, at], x_sem.at[i]))
        f_loads[-1].start()
        x_loads[-1].start()

    barrier = pltpu.get_barrier_semaphore()
    for dy, dx in PLANE:
        pl.semaphore_signal(barrier, inc=1, device_id=(plane_peer(dy, dx),), device_id_type=MESH)
    for dz in range(1, 8):
        pl.semaphore_signal(barrier, inc=1, device_id=(z_peer(dz),), device_id_type=MESH)
    pl.semaphore_signal(barrier, inc=1, device_id=(partner,), device_id_type=MESH)

    for copy in loads:
        copy.wait()
    q3 = jnp.concatenate(split(q_v[...], 3), axis=0)
    gq3 = jnp.concatenate(split(fold(nt(q3, g_v[...])) * (1.0 / 16.0), 3), axis=0)

    def term(c):
        f_loads[c].wait()
        x_loads[c].wait()
        at = pl.ds(pl.multiple_of(chunks[c] * CH, CH), CH)
        v = fold(nt(q3, f_v[at, :]) + nn(gq3, x_v[:, at]))
        for i in range(4):
            terms[c * 4 + i] = v[:, i * 128 : (i + 1) * 128]

    core_copies, plane_copies = {}, {}

    def to_core(c):
        at = pl.ds(c * 4, 4)
        core_copies[c] = send(
            terms.at[at, other], core_recv.at[at], core_ss.at[c], core_rs.at[c], partner
        )

    def to_plane(c):
        core_copies[c].wait_recv()
        at = pl.ds(c * 4, 4)
        acc[at] = terms[at, own, :] + core_recv[at]
        part, dy = c // 4, (c % 4 + 1) % 4
        for dx in range(4):
            d = dy * 4 + dx
            if d > 0:
                plane_copies[part, d] = send(
                    acc.at[c * 4 + lax.rem(x + dx, 4)], plane_recv.at[part, d],
                    plane_ss.at[part, d], plane_rs.at[part, d], plane_peer(dy, dx),
                )

    for c in range(4):
        term(c)
    pl.semaphore_wait(barrier, 23)
    for c in range(4):
        to_core(c)
    for c in range(4, 8):
        term(c)
        to_core(c)
        if c >= 5:
            to_plane(c - 5)
    for c in range(3, 8):
        to_plane(c)

    def matrix(i, carry):
        at = pl.ds(pl.multiple_of(i * CH, CH), CH)
        m_ref[at, :] = tn(x_v[:, at], g_v[...]) * (1.0 / 16.0) + f_v[at, :].astype(F32)
        return carry

    lax.fori_loop(0, D // CH, matrix, 0)

    z_copies = []
    for part in range(2):
        s = acc[part * 16 + 12 + x]
        for d in range(1, 16):
            plane_copies[part, d].wait_recv()
            s = s + plane_recv[part, d]
        z_group[part, z] = s
        mine = z_group.at[part, z]
        z_copies.append(
            [send(mine, mine, z_ss.at[part, dz], z_rs.at[part, dz], z_peer(dz)) for dz in range(1, 8)]
        )

    plane_gathers = {}
    for part in range(2):
        for copy in z_copies[part]:
            copy.wait_recv()
        s = z_group[part, 0]
        for k in range(1, 8):
            s = s + z_group[part, k]
        p_full[part * 16 + plane, own, :] = s
        mine = p_full.at[part * 16 + plane, own]
        for dy, dx in PLANE:
            d = dy * 4 + dx
            plane_gathers[part, d] = send(
                mine, mine, pg_ss.at[part, d], pg_rs.at[part, d], plane_peer(dy, dx)
            )

    def consume(c, first):
        p = p_full[pl.ds(c * 4, 4)]
        p = jnp.concatenate([p[i] for i in range(4)], axis=1)
        p1, p2, p3 = split(p, 3)
        p3 = jnp.concatenate([p1, p2, p3], axis=0)
        at = pl.ds(pl.multiple_of(c * CH, CH), CH)
        gram, yt, st = nt(p3, p3), nt(p3, x_v[:, at]), nn(p3, f_v[at, :])
        gram_v[...] = gram if first else gram_v[...] + gram
        y_v[...] = yt if first else y_v[...] + yt
        st_v[...] = st if first else st_v[...] + st
        pt_ref[at, :] = p3[0:128].T

    for part in range(2):
        core_gathers = {}
        for dy in (0, 1, 3, 2):
            for dx in range(4):
                if dy * 4 + dx > 0:
                    plane_gathers[part, dy * 4 + dx].wait_recv()
            rows = p_full.at[pl.ds(part * 16 + lax.rem(y + 4 - dy, 4) * 4, 4), own]
            core_gathers[dy] = send(rows, rows, cg_ss.at[part, dy], cg_rs.at[part, dy], partner)
        for dy in (0, 1, 3, 2):
            core_gathers[dy].wait_recv()
            consume(part * 4 + lax.rem(y + 4 - dy, 4), part == 0 and dy == 0)

    y3 = jnp.concatenate(split(fold(y_v[...]) * (1.0 / 16.0), 3), axis=0)
    s = fold(st_v[...] + nn(y3, g_v[...]))
    for p in range(16):
        s_send[p] = s[(p // 2) * 8 : (p // 2) * 8 + 8, (p % 2) * 256 : (p % 2) * 256 + 256]
    s1 = {}
    for dy, dx in PLANE:
        d = dy * 4 + dx
        to = lax.rem(y + dy, 4) * 4 + lax.rem(x + dx, 4)
        s1[d] = send(s_send.at[to], s_recv.at[d], s1_ss.at[d], s1_rs.at[d], plane_peer(dy, dx))

    gram = gram_v[...]
    gram = fold(gram)
    gram = (gram[:, 128:192] + gram[:, 64:128]) + gram[:, 0:64]
    rows = lax.broadcasted_iota(jnp.int32, (RANK, RANK), 0)
    cols = lax.broadcasted_iota(jnp.int32, (RANK, RANK), 1)
    eye = (rows == cols).astype(F32)
    a = jnp.concatenate([gram, eye], axis=1)
    a = eliminate(a, 0, 22)

    s = s_send[plane]
    for d in range(1, 16):
        s1[d].wait_recv()
        s = s + s_recv[d]
    s_group[z] = s
    mine = s_group.at[z]
    s2 = [send(mine, mine, s2_ss.at[dz], s2_rs.at[dz], z_peer(dz)) for dz in range(1, 8)]
    a = eliminate(a, 22, 43)
    for copy in s2:
        copy.wait_recv()
    s = s_group[0]
    for k in range(1, 8):
        s = s + s_group[k]
    s_core[0] = s
    copy = send(s_core.at[0], s_core.at[1], sc_ss, sc_rs, partner)
    copy.wait_recv()
    s_full[plane] = s + s_core[1]
    mine = s_full.at[plane]
    s3 = []
    for dy, dx in PLANE:
        d = dy * 4 + dx
        s3.append(send(mine, mine, s3_ss.at[d], s3_rs.at[d], plane_peer(dy, dx)))
    a = eliminate(a, 43, 64)
    diag = jnp.sum(a[:, 0:64] * eye, axis=1, keepdims=True)
    inv = a[:, 64:128] * (1.0 / jnp.sqrt(diag))
    inv_t = inv.T
    for copy in s3:
        copy.wait_recv()

    s = jnp.concatenate(
        [jnp.concatenate([s_full[2 * r], s_full[2 * r + 1]], axis=1) for r in range(8)], axis=0
    )
    qn = jnp.dot(inv, s, precision=HIGH, preferred_element_type=F32) * (1.0 / N_DP)
    w = jnp.dot(inv_t, qn, precision=HIGH, preferred_element_type=F32)
    w1, w2 = split(w, 2)
    w = jnp.concatenate([w1, w1, w2, w2], axis=0)
    w_ref[...] = w
    qn_ref[...] = qn
    p = pt_ref[pl.ds(pl.multiple_of(me * 16, 16), 16), :]
    upd_ref[...] = nn(jnp.concatenate([p, p], axis=1), w)
    for copy in started:
        copy.wait_send()


def finish(upd_v, qn_v, m_v, pt_v, w_v, upd_hbm, qn_hbm, out_hbm, out_v, small_sem, out_sem):
    small = [
        pltpu.make_async_copy(upd_v, upd_hbm, small_sem.at[0]),
        pltpu.make_async_copy(qn_v, qn_hbm, small_sem.at[1]),
    ]
    for copy in small:
        copy.start()
    w = w_v[...]
    copies = []
    for i in range(D // CH):
        at = pl.ds(i * CH, CH)
        p = pt_v[at, :]
        out_v[at, :] = (m_v[at, :] - nn(jnp.concatenate([p, p], axis=1), w)).astype(BF16)
        copies.append(pltpu.make_async_copy(out_v.at[at, :], out_hbm.at[at, :], out_sem.at[i]))
        copies[-1].start()
    for copy in small + copies:
        copy.wait()


def body(inputs, out_grads, feedback, q_start):
    dma = pltpu.SemaphoreType.DMA
    vmem = pltpu.VMEM
    in_vmem = pl.BlockSpec(memory_space=vmem)
    in_any = pl.BlockSpec(memory_space=pl.ANY)
    upd, qn, m, pt, w = pl.pallas_call(
        kernel,
        out_shape=(
            vmem((D // N_DP, KV), F32),
            vmem((RANK, KV), F32),
            vmem((D, KV), F32),
            vmem((D, 128), BF16),
            vmem((256, KV), BF16),
        ),
        in_specs=[in_any] * 4,
        out_specs=(in_vmem,) * 5,
        scratch_shapes=[
            vmem((TOK, D), BF16),
            vmem((TOK, KV), BF16),
            vmem((D, KV), BF16),
            vmem((RANK, KV), F32),
            vmem((32, RANK, 128), F32),
            vmem((32, RANK, 128), F32),
            vmem((32, HALF, 128), F32),
            vmem((32, HALF, 128), F32),
            vmem((2, 16, HALF, 128), F32),
            vmem((2, 8, HALF, 128), F32),
            vmem((192, 192), F32),
            vmem((192, KV), F32),
            vmem((192, TOK), F32),
            vmem((16, 8, 256), F32),
            vmem((16, 8, 256), F32),
            vmem((8, 8, 256), F32),
            vmem((2, 8, 256), F32),
            vmem((16, 8, 256), F32),
            dma((2,)), dma((8,)), dma((8,)),
            dma((8,)), dma((8,)), dma((2, 16)), dma((2, 16)), dma((2, 8)), dma((2, 8)),
            dma((2, 16)), dma((2, 16)), dma((2, 4)), dma((2, 4)),
            dma((16,)), dma((16,)), dma((8,)), dma((8,)), dma, dma, dma((16,)), dma((16,)),
        ],
        compiler_params=pltpu.CompilerParams(
            collective_id=0, has_side_effects=True, vmem_limit_bytes=52 * MIB
        ),
    )(inputs, out_grads, feedback, q_start.T)
    upd, qn, new_feedback = pl.pallas_call(
        finish,
        out_shape=(
            jax.ShapeDtypeStruct((D // N_DP, KV), F32),
            jax.ShapeDtypeStruct((RANK, KV), F32),
            jax.ShapeDtypeStruct((D, KV), BF16),
        ),
        in_specs=[in_vmem] * 5,
        out_specs=(in_any,) * 3,
        scratch_shapes=[vmem((D, KV), BF16), dma((2,)), dma((8,))],
        compiler_params=pltpu.CompilerParams(vmem_limit_bytes=16 * MIB),
    )(upd, qn, m, pt, w)
    return upd, qn.T, new_feedback


def solution(mesh):
    placed = (P("dp", None), P("dp", None), P("dp", None), P())
    return jax.shard_map(
        body,
        mesh=mesh,
        in_specs=placed,
        out_specs=(P("dp", None), P(), P("dp", None)),
        check_vma=False,
    )
```

time: 75.4 us -> 62 us (0.82)
  local copies, waits for them, and re-layouts: 9.42 us -> 0 us
  Pallas kernels: 65.2 us -> 61.3 us
    unnamed x7 -> x0, local copies, waits for them, and re-layouts: 8.65 us -> none
    pallas_call x1 -> x2, Pallas kernels: 65.2 us -> 61.3 us  [the longest x1 58.9 us: body(): pl.pallas_call(kernel, out_shape=(vmem((D // N_DP, KV), F32), vmem((RANK,...]
    pallas_call x1 -> x0, local copies, waits for them, and re-layouts: 0.77 us -> none  [body(): pl.pallas_call(kernel, out_shape=(jax.ShapeDtypeStruct((D // N_DP, KV), F...]
where the time goes in v2:
time: 62 us; the launch traced here: 61.9 us
  Pallas kernels  61.3 us (99%)
  between operations  0.64 us (1%)
    pallas_call x1, Pallas kernels, body(): pl.pallas_call(kernel, out_shape=(vmem((D // N_DP, KV), F32), vmem((RANK,...  58.9 us
    pallas_call x1, Pallas kernels, body(): pl.pallas_call(finish, out_shape=(jax.ShapeDtypeStruct((D // N_DP, KV), F...  2.39 us

profile of v2, /device:TPU:1, one launch (start us, length us, event | category | flops | bytes accessed | tf_op | source)
XLA Modules:
  0.0 61.9 jit_solution(14953269029542474386)
XLA Ops:
  0.6 58.9 %shard_map.67 = (f32[16,512]{1,0:T(8,128)S(1)}, f32[64,512]{1,0:T(8,128)S(1)}, f32[4096,512]{1,0:T(8,128)S(1)}, bf16[4096,128]{1,0:T(8,128)(2,1)S(1)}, bf16[256,512]{1,0:T(8,128)(2,1)S(1)}) custom-call(bf16[256,4096]{1,0:T(8,128)(2,1)} %x_hbm.1, bf16[256,512]{1,0:T(8,128)(2,1)} %g_hbm.1, bf16[4096,512]{1,0:T(8,128)(2,1)} %f_hbm.1, f32[64,512]{1,0:T(8,128)} %bitcast.2), custom_call_target="tpu_custom_call" | custom-call | tf_op jit(solution)/shard_map/pallas_call | solution.py:305
  59.5 2.4 %shard_map.68 = (f32[16,512]{1,0:T(8,128)}, f32[64,512]{1,0:T(8,128)}, bf16[4096,512]{1,0:T(8,128)(2,1)}) custom-call(f32[16,512]{1,0:T(8,128)S(1)} %get-tuple-element.11.upd_v, f32[64,512]{1,0:T(8,128)S(1)} %get-tuple-element.12.qn_v, f32[4096,512]{1,0:T(8,128)S(1)} %get-tuple-element.13.m_v, bf16[4096,128]{1,0:T(8,128)(2,1)S(1)} %get-tuple-element.14.pt_v, ...), custom_call_target="tpu_custom_call" | custom-call | tf_op jit(solution)/shard_map/pallas_call | solution.py:344

commit v3 on v2

v3 whole, which is shorter than its diff:
```python
import jax
import jax.numpy as jnp
from jax import lax
from jax.experimental import pallas as pl
from jax.experimental.pallas import tpu as pltpu
from jax.sharding import PartitionSpec as P

HIGH = lax.Precision.HIGHEST
MESH = pl.DeviceIdType.MESH
F32, BF16 = jnp.float32, jnp.bfloat16

D, KV, RANK, TOK, N_DP = 4096, 512, 64, 256, 256
HALF = RANK // 2
CH = 512
PARTS = 4
PART = D // PARTS
BLOCKS = PART // 128
ROWS = HALF // 2
PLANE = [(dy, dx) for dy in range(4) for dx in range(4) if (dy, dx) != (0, 0)]
MIB = 1024 * 1024


def nn(a, b):
    return lax.dot_general(a, b, (((1,), (0,)), ((), ())), preferred_element_type=F32)


def nt(a, b):
    return lax.dot_general(a, b, (((1,), (1,)), ((), ())), preferred_element_type=F32)


def tn(a, b):
    return lax.dot_general(a, b, (((0,), (0,)), ((), ())), preferred_element_type=F32)


def split(v, pieces):
    out = []
    for at in range(pieces):
        out.append(v.astype(BF16))
        if at < pieces - 1:
            v = v - out[-1].astype(F32)
    return out


def fold(t):
    out = t[-RANK:]
    for at in range(t.shape[0] - 2 * RANK, -1, -RANK):
        out = out + t[at : at + RANK]
    return out


def eliminate(a, first, last):
    rows = lax.broadcasted_iota(jnp.int32, (RANK, 1), 0)
    for k in range(first, last):
        row = a[k : k + 1, :]
        ratio = a[:, k : k + 1] / a[k : k + 1, k : k + 1]
        a = a - jnp.where(rows > k, ratio, 0.0) * row
    return a


def kernel(
    x_hbm, g_hbm, f_hbm, q_hbm, upd_ref, qn_ref, m_ref, pt_ref, w_ref,
    x_v, g_v, f_v, q_v, p_full,
    terms, core_recv, acc, plane_recv, z_group,
    st_v, y_v, s_send, s_recv, s_group, s_core, s_full,
    load_sem, send_sem, core_sem, plane_sem, z_sem, gather_sem, pair_sem, s_sem,
):
    me = lax.axis_index("dp")
    core = lax.rem(me, 2)
    z = lax.rem(lax.div(me, 2), 8)
    group = lax.rem(me, 16)
    plane = lax.div(me, 16)
    y, x = lax.div(plane, 4), lax.rem(plane, 4)
    partner = me + 1 - 2 * core
    own = pl.ds(pl.multiple_of(core * HALF, HALF), HALF)
    other = pl.ds(pl.multiple_of((1 - core) * HALF, HALF), HALF)

    def place(dy, dx):
        return lax.rem(y + dy, 4) * 4 + lax.rem(x + dx, 4)

    def plane_peer(dy, dx):
        return place(dy, dx) * 16 + group

    def z_peer(dz):
        return plane * 16 + lax.rem(z + dz, 8) * 2 + core

    def send(src, dst, ss, rs, device):
        pltpu.make_async_remote_copy(
            src_ref=src, dst_ref=dst, send_sem=ss, recv_sem=rs,
            device_id=(device,), device_id_type=MESH,
        ).start()

    def take(like, sem):
        pltpu.make_async_copy(like, like, sem).wait()

    loads = [
        pltpu.make_async_copy(q_hbm, q_v, load_sem.at[0]),
        pltpu.make_async_copy(g_hbm, g_v, load_sem.at[1]),
    ]
    for part in range(PARTS):
        at = pl.ds(part * PART, PART)
        loads.append(pltpu.make_async_copy(f_hbm.at[at, :], f_v.at[at, :], load_sem.at[2 + 2 * part]))
        loads.append(pltpu.make_async_copy(x_hbm.at[:, at], x_v.at[:, at], load_sem.at[3 + 2 * part]))
    for copy in loads:
        copy.start()

    barrier = pltpu.get_barrier_semaphore()
    for dy, dx in PLANE:
        pl.semaphore_signal(barrier, inc=1, device_id=(plane_peer(dy, dx),), device_id_type=MESH)
    for dz in range(1, 8):
        pl.semaphore_signal(barrier, inc=1, device_id=(z_peer(dz),), device_id_type=MESH)
    pl.semaphore_signal(barrier, inc=1, device_id=(partner,), device_id_type=MESH)

    for copy in loads[0:2]:
        copy.wait()
    q2 = jnp.concatenate(split(q_v[...], 2), axis=0)
    gq2 = jnp.concatenate(split(fold(nt(q2, g_v[...])) * (1.0 / 16.0), 2), axis=0)

    def term(part):
        for copy in loads[2 + 2 * part : 4 + 2 * part]:
            copy.wait()
        for c in range(part * PART // CH, (part + 1) * PART // CH):
            at = pl.ds(c * CH, CH)
            v = fold(nt(q2, f_v[at, :]) + nn(gq2, x_v[:, at]))
            for i in range(4):
                terms[c * 4 + i] = v[:, i * 128 : (i + 1) * 128]

    def to_core(part):
        at = pl.ds(part * BLOCKS, BLOCKS)
        send(terms.at[at, other], core_recv.at[at], send_sem.at[0], core_sem.at[part], partner)

    def piece(part, to):
        return part * BLOCKS + lax.div(to, 2), pl.ds(pl.multiple_of(lax.rem(to, 2) * ROWS, ROWS), ROWS)

    def to_plane(part):
        at = pl.ds(part * BLOCKS, BLOCKS)
        take(core_recv.at[at], core_sem.at[part])
        acc[at] = terms[at, own, :] + core_recv[at]
        for dy, dx in PLANE:
            send(
                acc.at[piece(part, place(dy, dx))], plane_recv.at[part, dy * 4 + dx],
                send_sem.at[1], plane_sem.at[part], plane_peer(dy, dx),
            )

    term(0)
    term(1)
    pl.semaphore_wait(barrier, 23)
    to_core(0)
    to_core(1)
    term(2)
    to_core(2)
    to_plane(0)
    term(3)
    to_core(3)
    for part in range(1, PARTS):
        to_plane(part)

    for c in range(D // CH):
        at = pl.ds(c * CH, CH)
        m_ref[at, :] = tn(x_v[:, at], g_v[...]) * (1.0 / 16.0) + f_v[at, :].astype(F32)

    for part in range(PARTS):
        if part == 3:
            pass
        take(plane_recv.at[part, pl.ds(1, 15)], plane_sem.at[part])
        block, rows = piece(part, plane)
        s = acc[block, rows, :]
        for d in range(1, 16):
            s = s + plane_recv[part, d]
        z_group[part, z] = s
        mine = z_group.at[part, z]
        for dz in range(1, 8):
            send(mine, mine, send_sem.at[2], z_sem.at[part], z_peer(dz))

    for part in range(PARTS):
        if part == 3:
            pass
        take(z_group.at[part, pl.ds(0, 7)], z_sem.at[part])
        s = z_group[part, 0]
        for k in range(1, 8):
            s = s + z_group[part, k]
        block = part * BLOCKS + lax.div(plane, 2)
        rows = pl.ds(pl.multiple_of(core * HALF + lax.rem(plane, 2) * ROWS, ROWS), ROWS)
        p_full[block, rows, :] = s
        mine = p_full.at[block, rows]
        for dy, dx in PLANE:
            send(mine, mine, send_sem.at[3], gather_sem.at[part], plane_peer(dy, dx))

    def pieces(c, count):
        p = p_full[pl.ds(c * 4, 4)]
        p = jnp.concatenate([p[i] for i in range(4)], axis=1)
        return jnp.concatenate(split(p, count), axis=0)

    def consume(part):
        yt, st = [], []
        for c in range(part * PART // CH, (part + 1) * PART // CH):
            p2 = pieces(c, 2)
            at = pl.ds(c * CH, CH)
            yt.append(nt(p2, x_v[:, at]))
            st.append(nn(p2, f_v[at, :]))
        yt, st = sum(yt[1:], yt[0]), sum(st[1:], st[0])
        y_v[...] = yt if part == 0 else y_v[...] + yt
        st_v[...] = st if part == 0 else st_v[...] + st

    for part in range(PARTS):
        if part == 3:
            pass
        take(plane_recv.at[part, pl.ds(1, 15)], gather_sem.at[part])
        rows = p_full.at[pl.ds(part * BLOCKS, BLOCKS), own]
        send(rows, rows, send_sem.at[4], pair_sem.at[part], partner)
        take(rows, pair_sem.at[part])
        consume(part)

    y2 = jnp.concatenate(split(fold(y_v[...]) * (1.0 / 16.0), 2), axis=0)
    s = fold(st_v[...] + nn(y2, g_v[...]))
    for p in range(16):
        s_send[p] = s[(p // 2) * 8 : (p // 2) * 8 + 8, (p % 2) * 256 : (p % 2) * 256 + 256]
    for dy, dx in PLANE:
        send(
            s_send.at[place(dy, dx)], s_recv.at[dy * 4 + dx],
            send_sem.at[5], s_sem.at[0], plane_peer(dy, dx),
        )

    gram = jnp.zeros((3 * RANK, 3 * RANK), F32)
    for c in range(8):
        p3 = pieces(c, 3)
        gram = gram + nt(p3, p3)
        pt_ref[c * CH : (c + 1) * CH, :] = p3[0:128].T
    gram = fold(gram)
    gram = (gram[:, 128:192] + gram[:, 64:128]) + gram[:, 0:64]
    rows = lax.broadcasted_iota(jnp.int32, (RANK, RANK), 0)
    cols = lax.broadcasted_iota(jnp.int32, (RANK, RANK), 1)
    eye = (rows == cols).astype(F32)
    a = jnp.concatenate([gram, eye], axis=1)
    a = eliminate(a, 0, 22)

    take(s_recv.at[pl.ds(1, 15)], s_sem.at[0])
    s = s_send[plane]
    for d in range(1, 16):
        s = s + s_recv[d]
    s_group[z] = s
    mine = s_group.at[z]
    for dz in range(1, 8):
        send(mine, mine, send_sem.at[6], s_sem.at[1], z_peer(dz))
    a = eliminate(a, 22, 43)
    take(s_group.at[pl.ds(0, 7)], s_sem.at[1])
    s = s_group[0]
    for k in range(1, 8):
        s = s + s_group[k]
    s_core[0] = s
    send(s_core.at[0], s_core.at[1], send_sem.at[7], s_sem.at[2], partner)
    take(s_core.at[1], s_sem.at[2])
    s_full[plane] = s + s_core[1]
    mine = s_full.at[plane]
    for dy, dx in PLANE:
        send(mine, mine, send_sem.at[8], s_sem.at[3], plane_peer(dy, dx))
    a = eliminate(a, 43, 64)
    diag = jnp.sum(a[:, 0:64] * eye, axis=1, keepdims=True)
    inv = a[:, 64:128] * (1.0 / jnp.sqrt(diag))
    inv_t = inv.T
    take(core_recv, send_sem.at[0])
    take(plane_recv.at[:, pl.ds(1, 15)], send_sem.at[1])
    take(z_group.at[:, pl.ds(0, 7)], send_sem.at[2])
    take(plane_recv.at[:, pl.ds(1, 15)], send_sem.at[3])
    take(core_recv, send_sem.at[4])
    take(s_recv.at[pl.ds(1, 15)], send_sem.at[5])
    take(s_group.at[pl.ds(0, 7)], send_sem.at[6])
    take(s_core.at[1], send_sem.at[7])
    take(s_recv.at[pl.ds(1, 15)], s_sem.at[3])

    s = jnp.concatenate(
        [jnp.concatenate([s_full[2 * r], s_full[2 * r + 1]], axis=1) for r in range(8)], axis=0
    )
    qn = jnp.dot(inv, s, precision=HIGH, preferred_element_type=F32) * (1.0 / N_DP)
    w = jnp.dot(inv_t, qn, precision=HIGH, preferred_element_type=F32)
    w1, w2 = split(w, 2)
    w = jnp.concatenate([w1, w1, w2, w2], axis=0)
    w_ref[...] = w
    qn_ref[...] = qn
    p = pt_ref[pl.ds(pl.multiple_of(me * 16, 16), 16), :]
    upd_ref[...] = nn(jnp.concatenate([p, p], axis=1), w)
    take(s_recv.at[pl.ds(1, 15)], send_sem.at[8])


def finish(upd_v, qn_v, m_v, pt_v, w_v, upd_hbm, qn_hbm, out_hbm, out_v, small_sem):
    small = [
        pltpu.make_async_copy(upd_v, upd_hbm, small_sem.at[0]),
        pltpu.make_async_copy(qn_v, qn_hbm, small_sem.at[1]),
    ]
    for copy in small:
        copy.start()
    w = w_v[...]
    for i in range(D // CH):
        at = pl.ds(i * CH, CH)
        p = pt_v[at, :]
        out_v[at, :] = (m_v[at, :] - nn(jnp.concatenate([p, p], axis=1), w)).astype(BF16)
        pltpu.make_async_copy(out_v.at[at, :], out_hbm.at[at, :], small_sem.at[2]).start()
    for copy in small:
        copy.wait()
    pltpu.make_async_copy(out_v, out_hbm, small_sem.at[2]).wait()


def body(inputs, out_grads, feedback, q_start):
    dma = pltpu.SemaphoreType.DMA
    vmem = pltpu.VMEM
    in_vmem = pl.BlockSpec(memory_space=vmem)
    in_any = pl.BlockSpec(memory_space=pl.ANY)
    upd, qn, m, pt, w = pl.pallas_call(
        kernel,
        out_shape=(
            vmem((D // N_DP, KV), F32),
            vmem((RANK, KV), F32),
            vmem((D, KV), F32),
            vmem((D, 128), BF16),
            vmem((256, KV), BF16),
        ),
        in_specs=[in_any] * 4,
        out_specs=(in_vmem,) * 5,
        scratch_shapes=[
            vmem((TOK, D), BF16),
            vmem((TOK, KV), BF16),
            vmem((D, KV), BF16),
            vmem((RANK, KV), F32),
            vmem((32, RANK, 128), F32),
            vmem((32, RANK, 128), F32),
            vmem((32, HALF, 128), F32),
            vmem((32, HALF, 128), F32),
            vmem((PARTS, 16, ROWS, 128), F32),
            vmem((PARTS, 8, ROWS, 128), F32),
            vmem((2 * RANK, KV), F32),
            vmem((2 * RANK, TOK), F32),
            vmem((16, 8, 256), F32),
            vmem((16, 8, 256), F32),
            vmem((8, 8, 256), F32),
            vmem((2, 8, 256), F32),
            vmem((16, 8, 256), F32),
            dma((2 + 2 * PARTS,)), dma((9,)), dma((PARTS,)), dma((PARTS,)),
            dma((PARTS,)), dma((PARTS,)), dma((PARTS,)), dma((4,)),
        ],
        compiler_params=pltpu.CompilerParams(
            collective_id=0, has_side_effects=True, vmem_limit_bytes=52 * MIB
        ),
    )(inputs, out_grads, feedback, q_start.T)
    upd, qn, new_feedback = pl.pallas_call(
        finish,
        out_shape=(
            jax.ShapeDtypeStruct((D // N_DP, KV), F32),
            jax.ShapeDtypeStruct((RANK, KV), F32),
            jax.ShapeDtypeStruct((D, KV), BF16),
        ),
        in_specs=[in_vmem] * 5,
        out_specs=(in_any,) * 3,
        scratch_shapes=[vmem((D, KV), BF16), dma((3,))],
        compiler_params=pltpu.CompilerParams(vmem_limit_bytes=16 * MIB),
    )(upd, qn, m, pt, w)
    return upd, qn.T, new_feedback


def solution(mesh):
    placed = (P("dp", None), P("dp", None), P("dp", None), P())
    return jax.shard_map(
        body,
        mesh=mesh,
        in_specs=placed,
        out_specs=(P("dp", None), P(), P("dp", None)),
        check_vma=False,
    )
```

time: 62 us -> 57 us (0.919)
  Pallas kernels: 61.3 us -> 56.3 us
    pallas_call x1, Pallas kernels: 58.9 us -> 53.9 us  [body(): pl.pallas_call(kernel, out_shape=(vmem((D // N_DP, KV), F32), vmem((RANK,...]
where the time goes in v3:
time: 57 us; the launch traced here: 56.9 us
  Pallas kernels  56.3 us (99%)
  between operations  0.64 us (1%)
    pallas_call x1, Pallas kernels, body(): pl.pallas_call(kernel, out_shape=(vmem((D // N_DP, KV), F32), vmem((RANK,...  53.9 us
    pallas_call x1, Pallas kernels, body(): pl.pallas_call(finish, out_shape=(jax.ShapeDtypeStruct((D // N_DP, KV), F...  2.33 us

profile of v3, /device:TPU:1, one launch (start us, length us, event | category | flops | bytes accessed | tf_op | source)
XLA Modules:
  0.0 56.9 jit_solution(3165514864875793191)
XLA Ops:
  0.6 53.9 %shard_map.67 = (f32[16,512]{1,0:T(8,128)S(1)}, f32[64,512]{1,0:T(8,128)S(1)}, f32[4096,512]{1,0:T(8,128)S(1)}, bf16[4096,128]{1,0:T(8,128)(2,1)S(1)}, bf16[256,512]{1,0:T(8,128)(2,1)S(1)}) custom-call(bf16[256,4096]{1,0:T(8,128)(2,1)} %x_hbm.1, bf16[256,512]{1,0:T(8,128)(2,1)} %g_hbm.1, bf16[4096,512]{1,0:T(8,128)(2,1)} %f_hbm.1, f32[64,512]{1,0:T(8,128)} %bitcast.2), custom_call_target="tpu_custom_call" | custom-call | tf_op jit(solution)/shard_map/pallas_call | solution.py:307
  54.6 2.3 %shard_map.68 = (f32[16,512]{1,0:T(8,128)}, f32[64,512]{1,0:T(8,128)}, bf16[4096,512]{1,0:T(8,128)(2,1)}) custom-call(f32[16,512]{1,0:T(8,128)S(1)} %get-tuple-element.11.upd_v, f32[64,512]{1,0:T(8,128)S(1)} %get-tuple-element.12.qn_v, f32[4096,512]{1,0:T(8,128)S(1)} %get-tuple-element.13.m_v, bf16[4096,128]{1,0:T(8,128)(2,1)S(1)} %get-tuple-element.14.pt_v, ...), custom_call_target="tpu_custom_call" | custom-call | tf_op jit(solution)/shard_map/pallas_call | solution.py:343

commit v4 on v3

--- a/solution.py
+++ b/solution.py
@@ -16,7 +16,7 @@
 PART = D // PARTS
 BLOCKS = PART // 128
 ROWS = HALF // 2
-PLANE = [(dy, dx) for dy in range(4) for dx in range(4) if (dy, dx) != (0, 0)]
+PLANE = [(2, 2), (2, 1), (2, 3), (1, 2), (3, 2), (1, 1), (1, 3), (3, 1), (3, 3), (2, 0), (0, 2), (0, 1), (0, 3), (1, 0), (3, 0)]
 MIB = 1024 * 1024
 
 
@@ -61,8 +61,8 @@
     x_hbm, g_hbm, f_hbm, q_hbm, upd_ref, qn_ref, m_ref, pt_ref, w_ref,
     x_v, g_v, f_v, q_v, p_full,
     terms, core_recv, acc, plane_recv, z_group,
-    st_v, y_v, s_send, s_recv, s_group, s_core, s_full,
-    load_sem, send_sem, core_sem, plane_sem, z_sem, gather_sem, pair_sem, s_sem,
+    m_peer, m_chip, st_v, s_send, s_recv, s_group, s_full,
+    load_sem, send_sem, core_sem, plane_sem, z_sem, gather_sem, pair_sem, s_sem, peer_sem,
 ):
     me = lax.axis_index("dp")
     core = lax.rem(me, 2)
@@ -104,10 +104,10 @@
         copy.start()
 
     barrier = pltpu.get_barrier_semaphore()
+    for dz in (4, 3, 5, 2, 6, 1, 7):
+        pl.semaphore_signal(barrier, inc=1, device_id=(z_peer(dz),), device_id_type=MESH)
     for dy, dx in PLANE:
         pl.semaphore_signal(barrier, inc=1, device_id=(plane_peer(dy, dx),), device_id_type=MESH)
-    for dz in range(1, 8):
-        pl.semaphore_signal(barrier, inc=1, device_id=(z_peer(dz),), device_id_type=MESH)
     pl.semaphore_signal(barrier, inc=1, device_id=(partner,), device_id_type=MESH)
 
     for copy in loads[0:2]:
@@ -142,9 +142,9 @@
             )
 
     term(0)
-    term(1)
     pl.semaphore_wait(barrier, 23)
     to_core(0)
+    term(1)
     to_core(1)
     term(2)
     to_core(2)
@@ -154,9 +154,19 @@
     for part in range(1, PARTS):
         to_plane(part)
 
-    for c in range(D // CH):
-        at = pl.ds(c * CH, CH)
-        m_ref[at, :] = tn(x_v[:, at], g_v[...]) * (1.0 / 16.0) + f_v[at, :].astype(F32)
+    for part in range(PARTS):
+        for c in range(part * PART // CH, (part + 1) * PART // CH):
+            at = pl.ds(c * CH, CH)
+            m_ref[at, :] = tn(x_v[:, at], g_v[...]) * (1.0 / 16.0) + f_v[at, :].astype(F32)
+        at = pl.ds(part * PART, PART)
+        send(m_ref.at[at], m_peer.at[at], send_sem.at[8], peer_sem.at[part], partner)
+
+    def chip(part):
+        at = pl.ds(part * PART, PART)
+        take(m_peer.at[at], peer_sem.at[part])
+        m1, m2 = split(m_ref[at, :] + m_peer[at, :], 2)
+        m_chip[0, at, :] = m1
+        m_chip[1, at, :] = m2
 
     for part in range(PARTS):
         if part == 3:
@@ -171,6 +181,8 @@
         for dz in range(1, 8):
             send(mine, mine, send_sem.at[2], z_sem.at[part], z_peer(dz))
 
+    chip(0)
+    chip(1)
     for part in range(PARTS):
         if part == 3:
             pass
@@ -191,35 +203,40 @@
         return jnp.concatenate(split(p, count), axis=0)
 
     def consume(part):
-        yt, st = [], []
-        for c in range(part * PART // CH, (part + 1) * PART // CH):
-            p2 = pieces(c, 2)
-            at = pl.ds(c * CH, CH)
-            yt.append(nt(p2, x_v[:, at]))
-            st.append(nn(p2, f_v[at, :]))
-        yt, st = sum(yt[1:], yt[0]), sum(st[1:], st[0])
-        y_v[...] = yt if part == 0 else y_v[...] + yt
-        st_v[...] = st if part == 0 else st_v[...] + st
-
-    for part in range(PARTS):
-        if part == 3:
-            pass
+        blocks = p_full[pl.ds(part * BLOCKS, BLOCKS), own, :]
+        near, far = [], []
+        for c in range(PART // CH):
+            p = jnp.concatenate([blocks[c * 4 + i] for i in range(4)], axis=1)
+            p1, p2 = split(p, 2)
+            at = pl.ds(part * PART + c * CH, CH)
+            near.append(nn(jnp.concatenate([p1, p2], axis=0), m_chip[0, at, :]))
+            far.append(nn(p1, m_chip[1, at, :]))
+        near, far = sum(near[1:], near[0]), sum(far[1:], far[0])
+        total = (far + near[HALF:]) + near[:HALF]
+        st_v[...] = total if part == 0 else st_v[...] + total
+
+    def forward(part):
         take(plane_recv.at[part, pl.ds(1, 15)], gather_sem.at[part])
         rows = p_full.at[pl.ds(part * BLOCKS, BLOCKS), own]
         send(rows, rows, send_sem.at[4], pair_sem.at[part], partner)
-        take(rows, pair_sem.at[part])
+
+    chip(2)
+    chip(3)
+    for part in range(PARTS):
+        forward(part)
         consume(part)
 
-    y2 = jnp.concatenate(split(fold(y_v[...]) * (1.0 / 16.0), 2), axis=0)
-    s = fold(st_v[...] + nn(y2, g_v[...]))
+    s = st_v[...]
     for p in range(16):
-        s_send[p] = s[(p // 2) * 8 : (p // 2) * 8 + 8, (p % 2) * 256 : (p % 2) * 256 + 256]
+        s_send[p] = s[(p // 4) * 8 : (p // 4) * 8 + 8, (p % 4) * 128 : (p % 4) * 128 + 128]
     for dy, dx in PLANE:
         send(
             s_send.at[place(dy, dx)], s_recv.at[dy * 4 + dx],
             send_sem.at[5], s_sem.at[0], plane_peer(dy, dx),
         )
 
+    for part in range(PARTS):
+        take(p_full.at[pl.ds(part * BLOCKS, BLOCKS), own], pair_sem.at[part])
     gram = jnp.zeros((3 * RANK, 3 * RANK), F32)
     for c in range(8):
         p3 = pieces(c, 3)
@@ -231,7 +248,7 @@
     cols = lax.broadcasted_iota(jnp.int32, (RANK, RANK), 1)
     eye = (rows == cols).astype(F32)
     a = jnp.concatenate([gram, eye], axis=1)
-    a = eliminate(a, 0, 22)
+    a = eliminate(a, 0, 8)
 
     take(s_recv.at[pl.ds(1, 15)], s_sem.at[0])
     s = s_send[plane]
@@ -241,19 +258,19 @@
     mine = s_group.at[z]
     for dz in range(1, 8):
         send(mine, mine, send_sem.at[6], s_sem.at[1], z_peer(dz))
-    a = eliminate(a, 22, 43)
+    a = eliminate(a, 8, 36)
     take(s_group.at[pl.ds(0, 7)], s_sem.at[1])
     s = s_group[0]
     for k in range(1, 8):
         s = s + s_group[k]
-    s_core[0] = s
-    send(s_core.at[0], s_core.at[1], send_sem.at[7], s_sem.at[2], partner)
-    take(s_core.at[1], s_sem.at[2])
-    s_full[plane] = s + s_core[1]
-    mine = s_full.at[plane]
+    tile = core * 16 + plane
+    s_full[tile] = s
+    mine = s_full.at[tile]
     for dy, dx in PLANE:
-        send(mine, mine, send_sem.at[8], s_sem.at[3], plane_peer(dy, dx))
-    a = eliminate(a, 43, 64)
+        send(mine, mine, send_sem.at[7], s_sem.at[2], plane_peer(dy, dx))
+        send(mine, mine, send_sem.at[7], s_sem.at[2], plane_peer(dy, dx) + partner - me)
+    send(mine, mine, send_sem.at[7], s_sem.at[2], partner)
+    a = eliminate(a, 36, 64)
     diag = jnp.sum(a[:, 0:64] * eye, axis=1, keepdims=True)
     inv = a[:, 64:128] * (1.0 / jnp.sqrt(diag))
     inv_t = inv.T
@@ -264,11 +281,12 @@
     take(core_recv, send_sem.at[4])
     take(s_recv.at[pl.ds(1, 15)], send_sem.at[5])
     take(s_group.at[pl.ds(0, 7)], send_sem.at[6])
-    take(s_core.at[1], send_sem.at[7])
-    take(s_recv.at[pl.ds(1, 15)], s_sem.at[3])
+    take(m_peer, send_sem.at[8])
+    take(s_full.at[pl.ds(0, 31)], s_sem.at[2])
 
     s = jnp.concatenate(
-        [jnp.concatenate([s_full[2 * r], s_full[2 * r + 1]], axis=1) for r in range(8)], axis=0
+        [jnp.concatenate([s_full[4 * r + i] for i in range(4)], axis=1) for r in range(8)],
+        axis=0,
     )
     qn = jnp.dot(inv, s, precision=HIGH, preferred_element_type=F32) * (1.0 / N_DP)
     w = jnp.dot(inv_t, qn, precision=HIGH, preferred_element_type=F32)
@@ -278,7 +296,7 @@
     qn_ref[...] = qn
     p = pt_ref[pl.ds(pl.multiple_of(me * 16, 16), 16), :]
     upd_ref[...] = nn(jnp.concatenate([p, p], axis=1), w)
-    take(s_recv.at[pl.ds(1, 15)], send_sem.at[8])
+    take(s_full.at[pl.ds(0, 31)], send_sem.at[7])
 
 
 def finish(upd_v, qn_v, m_v, pt_v, w_v, upd_hbm, qn_hbm, out_hbm, out_v, small_sem):
@@ -326,15 +344,15 @@
             vmem((32, HALF, 128), F32),
             vmem((PARTS, 16, ROWS, 128), F32),
             vmem((PARTS, 8, ROWS, 128), F32),
-            vmem((2 * RANK, KV), F32),
-            vmem((2 * RANK, TOK), F32),
-            vmem((16, 8, 256), F32),
-            vmem((16, 8, 256), F32),
-            vmem((8, 8, 256), F32),
-            vmem((2, 8, 256), F32),
-            vmem((16, 8, 256), F32),
+            vmem((D, KV), F32),
+            vmem((2, D, KV), BF16),
+            vmem((HALF, KV), F32),
+            vmem((16, 8, 128), F32),
+            vmem((16, 8, 128), F32),
+            vmem((8, 8, 128), F32),
+            vmem((32, 8, 128), F32),
             dma((2 + 2 * PARTS,)), dma((9,)), dma((PARTS,)), dma((PARTS,)),
-            dma((PARTS,)), dma((PARTS,)), dma((PARTS,)), dma((4,)),
+            dma((PARTS,)), dma((PARTS,)), dma((PARTS,)), dma((3,)), dma((PARTS,)),
         ],
         compiler_params=pltpu.CompilerParams(
             collective_id=0, has_side_effects=True, vmem_limit_bytes=52 * MIB

time: 57 us -> 54.1 us (0.949)
  Pallas kernels: 56.3 us -> 53.4 us
    pallas_call x1, Pallas kernels: 53.9 us -> 51 us  [body(): pl.pallas_call(kernel, out_shape=(vmem((D // N_DP, KV), F32), vmem((RANK,...]
where the time goes in v4:
time: 54.1 us; the launch traced here: 54 us
  Pallas kernels  53.4 us (99%)
  between operations  0.64 us (1%)
    pallas_call x1, Pallas kernels, body(): pl.pallas_call(kernel, out_shape=(vmem((D // N_DP, KV), F32), vmem((RANK,...  51 us
    pallas_call x1, Pallas kernels, body(): pl.pallas_call(finish, out_shape=(jax.ShapeDtypeStruct((D // N_DP, KV), F...  2.33 us

profile of v4, /device:TPU:1, one launch (start us, length us, event | category | flops | bytes accessed | tf_op | source)
XLA Modules:
  0.0 54.0 jit_solution(10648789232779187997)
XLA Ops:
  0.6 51.0 %shard_map.67 = (f32[16,512]{1,0:T(8,128)S(1)}, f32[64,512]{1,0:T(8,128)S(1)}, f32[4096,512]{1,0:T(8,128)S(1)}, bf16[4096,128]{1,0:T(8,128)(2,1)S(1)}, bf16[256,512]{1,0:T(8,128)(2,1)S(1)}) custom-call(bf16[256,4096]{1,0:T(8,128)(2,1)} %x_hbm.1, bf16[256,512]{1,0:T(8,128)(2,1)} %g_hbm.1, bf16[4096,512]{1,0:T(8,128)(2,1)} %f_hbm.1, f32[64,512]{1,0:T(8,128)} %bitcast.2), custom_call_target="tpu_custom_call" | custom-call | tf_op jit(solution)/shard_map/pallas_call | solution.py:325
  51.7 2.3 %shard_map.68 = (f32[16,512]{1,0:T(8,128)}, f32[64,512]{1,0:T(8,128)}, bf16[4096,512]{1,0:T(8,128)(2,1)}) custom-call(f32[16,512]{1,0:T(8,128)S(1)} %get-tuple-element.11.upd_v, f32[64,512]{1,0:T(8,128)S(1)} %get-tuple-element.12.qn_v, f32[4096,512]{1,0:T(8,128)S(1)} %get-tuple-element.13.m_v, bf16[4096,128]{1,0:T(8,128)(2,1)S(1)} %get-tuple-element.14.pt_v, ...), custom_call_target="tpu_custom_call" | custom-call | tf_op jit(solution)/shard_map/pallas_call | solution.py:361

commit v5 on v4

--- a/solution.py
+++ b/solution.py
@@ -12,10 +12,11 @@
 D, KV, RANK, TOK, N_DP = 4096, 512, 64, 256, 256
 HALF = RANK // 2
 CH = 512
-PARTS = 4
-PART = D // PARTS
-BLOCKS = PART // 128
-ROWS = HALF // 2
+CHUNKS = (2, 2, 2, 2)
+PARTS = len(CHUNKS)
+FIRST = [sum(CHUNKS[:part]) for part in range(PARTS)]
+MPARTS = 4
+MPART = D // MPARTS
 PLANE = [(2, 2), (2, 1), (2, 3), (1, 2), (3, 2), (1, 1), (1, 3), (3, 1), (3, 3), (2, 0), (0, 2), (0, 1), (0, 3), (1, 0), (3, 0)]
 MIB = 1024 * 1024
 
@@ -92,12 +93,30 @@
     def take(like, sem):
         pltpu.make_async_copy(like, like, sem).wait()
 
+    def span(part):
+        return pl.ds(FIRST[part] * CH, CHUNKS[part] * CH)
+
+    def blocks(part):
+        return pl.ds(FIRST[part] * 4, CHUNKS[part] * 4)
+
+    def rows_of(part):
+        return 8 * CHUNKS[part]
+
+    def piece(part, to, base):
+        rows = rows_of(part)
+        per = HALF // rows
+        block = FIRST[part] * 4 + lax.div(to, per)
+        return block, pl.ds(pl.multiple_of(base + lax.rem(to, per) * rows, 8), rows)
+
+    def slots(ref, part, first, count):
+        return ref.at[part, pl.ds(first, count), pl.ds(0, rows_of(part))]
+
     loads = [
         pltpu.make_async_copy(q_hbm, q_v, load_sem.at[0]),
         pltpu.make_async_copy(g_hbm, g_v, load_sem.at[1]),
     ]
     for part in range(PARTS):
-        at = pl.ds(part * PART, PART)
+        at = span(part)
         loads.append(pltpu.make_async_copy(f_hbm.at[at, :], f_v.at[at, :], load_sem.at[2 + 2 * part]))
         loads.append(pltpu.make_async_copy(x_hbm.at[:, at], x_v.at[:, at], load_sem.at[3 + 2 * part]))
     for copy in loads:
@@ -118,82 +137,84 @@
     def term(part):
         for copy in loads[2 + 2 * part : 4 + 2 * part]:
             copy.wait()
-        for c in range(part * PART // CH, (part + 1) * PART // CH):
+        for c in range(FIRST[part], FIRST[part] + CHUNKS[part]):
             at = pl.ds(c * CH, CH)
             v = fold(nt(q2, f_v[at, :]) + nn(gq2, x_v[:, at]))
             for i in range(4):
                 terms[c * 4 + i] = v[:, i * 128 : (i + 1) * 128]
 
     def to_core(part):
-        at = pl.ds(part * BLOCKS, BLOCKS)
+        at = blocks(part)
         send(terms.at[at, other], core_recv.at[at], send_sem.at[0], core_sem.at[part], partner)
 
-    def piece(part, to):
-        return part * BLOCKS + lax.div(to, 2), pl.ds(pl.multiple_of(lax.rem(to, 2) * ROWS, ROWS), ROWS)
-
     def to_plane(part):
-        at = pl.ds(part * BLOCKS, BLOCKS)
+        at = blocks(part)
         take(core_recv.at[at], core_sem.at[part])
         acc[at] = terms[at, own, :] + core_recv[at]
         for dy, dx in PLANE:
             send(
-                acc.at[piece(part, place(dy, dx))], plane_recv.at[part, dy * 4 + dx],
+                acc.at[piece(part, place(dy, dx), 0)],
+                plane_recv.at[part, dy * 4 + dx, pl.ds(0, rows_of(part))],
                 send_sem.at[1], plane_sem.at[part], plane_peer(dy, dx),
             )
+
+    def matrix(part):
+        at = pl.ds(part * MPART, MPART)
+        for c in range(part * MPART // CH, (part + 1) * MPART // CH):
+            rows = pl.ds(c * CH, CH)
+            m_ref[rows, :] = tn(x_v[:, rows], g_v[...]) * (1.0 / 16.0) + f_v[rows, :].astype(F32)
+        send(m_ref.at[at], m_peer.at[at], send_sem.at[8], peer_sem.at[part], partner)
 
     term(0)
     pl.semaphore_wait(barrier, 23)
     to_core(0)
-    term(1)
-    to_core(1)
-    term(2)
-    to_core(2)
-    to_plane(0)
-    term(3)
-    to_core(3)
     for part in range(1, PARTS):
-        to_plane(part)
-
-    for part in range(PARTS):
-        for c in range(part * PART // CH, (part + 1) * PART // CH):
-            at = pl.ds(c * CH, CH)
-            m_ref[at, :] = tn(x_v[:, at], g_v[...]) * (1.0 / 16.0) + f_v[at, :].astype(F32)
-        at = pl.ds(part * PART, PART)
-        send(m_ref.at[at], m_peer.at[at], send_sem.at[8], peer_sem.at[part], partner)
+        term(part)
+        to_core(part)
+        if part >= 2:
+            to_plane(part - 2)
+    matrix(0)
+    to_plane(PARTS - 2)
+    matrix(1)
+    to_plane(PARTS - 1)
+    take(core_recv, send_sem.at[0])
+    for part in range(2, MPARTS):
+        matrix(part)
 
     def chip(part):
-        at = pl.ds(part * PART, PART)
+        at = pl.ds(part * MPART, MPART)
         take(m_peer.at[at], peer_sem.at[part])
         m1, m2 = split(m_ref[at, :] + m_peer[at, :], 2)
         m_chip[0, at, :] = m1
         m_chip[1, at, :] = m2
 
     for part in range(PARTS):
-        if part == 3:
+        if part == PARTS - 1:
             pass
-        take(plane_recv.at[part, pl.ds(1, 15)], plane_sem.at[part])
-        block, rows = piece(part, plane)
-        s = acc[block, rows, :]
+        take(slots(plane_recv, part, 1, 15), plane_sem.at[part])
+        rows = pl.ds(0, rows_of(part))
+        block, at = piece(part, plane, 0)
+        s = acc[block, at, :]
         for d in range(1, 16):
-            s = s + plane_recv[part, d]
-        z_group[part, z] = s
-        mine = z_group.at[part, z]
+            s = s + plane_recv[part, d, rows, :]
+        z_group[part, z, rows, :] = s
+        mine = z_group.at[part, z, rows]
         for dz in range(1, 8):
             send(mine, mine, send_sem.at[2], z_sem.at[part], z_peer(dz))
 
     chip(0)
     chip(1)
     for part in range(PARTS):
-        if part == 3:
+        if part == PARTS - 1:
             pass
-        take(z_group.at[part, pl.ds(0, 7)], z_sem.at[part])
-        s = z_group[part, 0]
+        take(slots(z_group, part, 0, 7), z_sem.at[part])
+        rows = pl.ds(0, rows_of(part))
+        s = z_group[part, 0, rows, :]
         for k in range(1, 8):
-            s = s + z_group[part, k]
-        block = part * BLOCKS + lax.div(plane, 2)
-        rows = pl.ds(pl.multiple_of(core * HALF + lax.rem(plane, 2) * ROWS, ROWS), ROWS)
-        p_full[block, rows, :] = s
-        mine = p_full.at[block, rows]
+            s = s + z_group[part, k, rows, :]
+        block, at = piece(part, plane, core * HALF)
+        p_full[block, at, :] = s
+        mine = p_full.at[block, at]
         for dy, dx in PLANE:
             send(mine, mine, send_sem.at[3], gather_sem.at[part], plane_peer(dy, dx))
 
@@ -203,12 +224,12 @@
         return jnp.concatenate(split(p, count), axis=0)
 
     def consume(part):
-        blocks = p_full[pl.ds(part * BLOCKS, BLOCKS), own, :]
+        held = p_full[blocks(part), own, :]
         near, far = [], []
-        for c in range(PART // CH):
-            p = jnp.concatenate([blocks[c * 4 + i] for i in range(4)], axis=1)
+        for c in range(CHUNKS[part]):
+            p = jnp.concatenate([held[c * 4 + i] for i in range(4)], axis=1)
             p1, p2 = split(p, 2)
-            at = pl.ds(part * PART + c * CH, CH)
+            at = pl.ds((FIRST[part] + c) * CH, CH)
             near.append(nn(jnp.concatenate([p1, p2], axis=0), m_chip[0, at, :]))
             far.append(nn(p1, m_chip[1, at, :]))
         near, far = sum(near[1:], near[0]), sum(far[1:], far[0])
@@ -216,15 +237,22 @@
         st_v[...] = total if part == 0 else st_v[...] + total
 
     def forward(part):
-        take(plane_recv.at[part, pl.ds(1, 15)], gather_sem.at[part])
-        rows = p_full.at[pl.ds(part * BLOCKS, BLOCKS), own]
+        take(slots(plane_recv, part, 1, 15), gather_sem.at[part])
+        rows = p_full.at[blocks(part), own]
         send(rows, rows, send_sem.at[4], pair_sem.at[part], partner)
+        if part >= PARTS - 4:
+            ref, sem = (
+                (core_recv.at[pl.ds(0, 30)], 1), (core_recv.at[pl.ds(0, 14)], 2),
+                (m_peer, 8), (core_recv.at[pl.ds(0, 30)], 3),
+            )[part - PARTS + 4]
+            take(ref, send_sem.at[sem])
 
     chip(2)
-    chip(3)
     for part in range(PARTS):
         forward(part)
         consume(part)
+        if FIRST[part + 1 : part + 2] == [4]:
+            chip(3)
 
     s = st_v[...]
     for p in range(16):
@@ -236,7 +264,7 @@
         )
 
     for part in range(PARTS):
-        take(p_full.at[pl.ds(part * BLOCKS, BLOCKS), own], pair_sem.at[part])
+        take(p_full.at[blocks(part), own], pair_sem.at[part])
     gram = jnp.zeros((3 * RANK, 3 * RANK), F32)
     for c in range(8):
         p3 = pieces(c, 3)
@@ -254,38 +282,35 @@
     s = s_send[plane]
     for d in range(1, 16):
         s = s + s_recv[d]
-    s_group[z] = s
-    mine = s_group.at[z]
-    for dz in range(1, 8):
+    s_group[core, z] = s
+    mine = s_group.at[core, z]
+    for dz in (4, 3, 5, 2, 6, 1, 7):
         send(mine, mine, send_sem.at[6], s_sem.at[1], z_peer(dz))
+        send(mine, mine, send_sem.at[6], s_sem.at[1], z_peer(dz) + partner - me)
+    send(mine, mine, send_sem.at[6], s_sem.at[1], partner)
+    take(core_recv, send_sem.at[4])
     a = eliminate(a, 8, 36)
-    take(s_group.at[pl.ds(0, 7)], s_sem.at[1])
-    s = s_group[0]
+    take(s_recv.at[pl.ds(1, 15)], s_sem.at[1])
+    s = s_group[:, 0]
     for k in range(1, 8):
-        s = s + s_group[k]
-    tile = core * 16 + plane
-    s_full[tile] = s
-    mine = s_full.at[tile]
+        s = s + s_group[:, k]
+    s_full[plane] = s
+    mine = s_full.at[plane]
     for dy, dx in PLANE:
         send(mine, mine, send_sem.at[7], s_sem.at[2], plane_peer(dy, dx))
-        send(mine, mine, send_sem.at[7], s_sem.at[2], plane_peer(dy, dx) + partner - me)
-    send(mine, mine, send_sem.at[7], s_sem.at[2], partner)
+    take(s_recv.at[pl.ds(1, 15)], send_sem.at[5])
     a = eliminate(a, 36, 64)
     diag = jnp.sum(a[:, 0:64] * eye, axis=1, keepdims=True)
     inv = a[:, 64:128] * (1.0 / jnp.sqrt(diag))
     inv_t = inv.T
-    take(core_recv, send_sem.at[0])
-    take(plane_recv.at[:, pl.ds(1, 15)], send_sem.at[1])
-    take(z_group.at[:, pl.ds(0, 7)], send_sem.at[2])
-    take(plane_recv.at[:, pl.ds(1, 15)], send_sem.at[3])
-    take(core_recv, send_sem.at[4])
-    take(s_recv.at[pl.ds(1, 15)], send_sem.at[5])
-    take(s_group.at[pl.ds(0, 7)], send_sem.at[6])
-    take(m_peer, send_sem.at[8])
-    take(s_full.at[pl.ds(0, 31)], s_sem.at[2])
+    take(s_full.at[pl.ds(1, 15)], s_sem.at[2])
 
     s = jnp.concatenate(
-        [jnp.concatenate([s_full[4 * r + i] for i in range(4)], axis=1) for r in range(8)],
+        [
+            jnp.concatenate([s_full[4 * r + i, half] for i in range(4)], axis=1)
+            for half in range(2)
+            for r in range(4)
+        ],
         axis=0,
     )
     qn = jnp.dot(inv, s, precision=HIGH, preferred_element_type=F32) * (1.0 / N_DP)
@@ -296,7 +321,8 @@
     qn_ref[...] = qn
     p = pt_ref[pl.ds(pl.multiple_of(me * 16, 16), 16), :]
     upd_ref[...] = nn(jnp.concatenate([p, p], axis=1), w)
-    take(s_full.at[pl.ds(0, 31)], send_sem.at[7])
+    take(s_recv.at[pl.ds(1, 15)], send_sem.at[6])
+    take(s_full.at[pl.ds(1, 15)], send_sem.at[7])
 
 
 def finish(upd_v, qn_v, m_v, pt_v, w_v, upd_hbm, qn_hbm, out_hbm, out_v, small_sem):
@@ -342,17 +368,17 @@
             vmem((32, RANK, 128), F32),
             vmem((32, HALF, 128), F32),
             vmem((32, HALF, 128), F32),
-            vmem((PARTS, 16, ROWS, 128), F32),
-            vmem((PARTS, 8, ROWS, 128), F32),
+            vmem((PARTS, 16, 8 * max(CHUNKS), 128), F32),
+            vmem((PARTS, 8, 8 * max(CHUNKS), 128), F32),
             vmem((D, KV), F32),
             vmem((2, D, KV), BF16),
             vmem((HALF, KV), F32),
             vmem((16, 8, 128), F32),
             vmem((16, 8, 128), F32),
-            vmem((8, 8, 128), F32),
-            vmem((32, 8, 128), F32),
+            vmem((2, 8, 8, 128), F32),
+            vmem((16, 2, 8, 128), F32),
             dma((2 + 2 * PARTS,)), dma((9,)), dma((PARTS,)), dma((PARTS,)),
-            dma((PARTS,)), dma((PARTS,)), dma((PARTS,)), dma((3,)), dma((PARTS,)),
+            dma((PARTS,)), dma((PARTS,)), dma((PARTS,)), dma((3,)), dma((MPARTS,)),
         ],
         compiler_params=pltpu.CompilerParams(
             collective_id=0, has_side_effects=True, vmem_limit_bytes=52 * MIB

time: 54.1 us -> 49.2 us (0.909)
  Pallas kernels: 53.4 us -> 48.5 us
    pallas_call x1, Pallas kernels: 51 us -> 46.2 us  [body(): pl.pallas_call(kernel, out_shape=(vmem((D // N_DP, KV), F32), vmem((RANK,...]
where the time goes in v5:
time: 49.2 us; the launch traced here: 49.1 us
  Pallas kernels  48.5 us (99%)
  between operations  0.64 us (1%)
    pallas_call x1, Pallas kernels, body(): pl.pallas_call(kernel, out_shape=(vmem((D // N_DP, KV), F32), vmem((RANK,...  46.2 us
    pallas_call x1, Pallas kernels, body(): pl.pallas_call(finish, out_shape=(jax.ShapeDtypeStruct((D // N_DP, KV), F...  2.33 us

profile of v5, /device:TPU:1, one launch (start us, length us, event | category | flops | bytes accessed | tf_op | source)
XLA Modules:
  0.0 49.1 jit_solution(16301057016721592782)
XLA Ops:
  0.6 46.2 %shard_map.67 = (f32[16,512]{1,0:T(8,128)S(1)}, f32[64,512]{1,0:T(8,128)S(1)}, f32[4096,512]{1,0:T(8,128)S(1)}, bf16[4096,128]{1,0:T(8,128)(2,1)S(1)}, bf16[256,512]{1,0:T(8,128)(2,1)S(1)}) custom-call(bf16[256,4096]{1,0:T(8,128)(2,1)} %x_hbm.1, bf16[256,512]{1,0:T(8,128)(2,1)} %g_hbm.1, bf16[4096,512]{1,0:T(8,128)(2,1)} %f_hbm.1, f32[64,512]{1,0:T(8,128)} %bitcast.2), custom_call_target="tpu_custom_call" | custom-call | tf_op jit(solution)/shard_map/pallas_call | solution.py:351
  46.8 2.3 %shard_map.68 = (f32[16,512]{1,0:T(8,128)}, f32[64,512]{1,0:T(8,128)}, bf16[4096,512]{1,0:T(8,128)(2,1)}) custom-call(f32[16,512]{1,0:T(8,128)S(1)} %get-tuple-element.11.upd_v, f32[64,512]{1,0:T(8,128)S(1)} %get-tuple-element.12.qn_v, f32[4096,512]{1,0:T(8,128)S(1)} %get-tuple-element.13.m_v, bf16[4096,128]{1,0:T(8,128)(2,1)S(1)} %get-tuple-element.14.pt_v, ...), custom_call_target="tpu_custom_call" | custom-call | tf_op jit(solution)/shard_map/pallas_call | solution.py:387

commit v6 on v5

--- a/solution.py
+++ b/solution.py
@@ -5,7 +5,6 @@
 from jax.experimental.pallas import tpu as pltpu
 from jax.sharding import PartitionSpec as P
 
-HIGH = lax.Precision.HIGHEST
 MESH = pl.DeviceIdType.MESH
 F32, BF16 = jnp.float32, jnp.bfloat16
 
@@ -49,6 +48,16 @@
     return out
 
 
+def beside(v):
+    v1, v2, v3 = split(v, 3)
+    return jnp.concatenate([v1, v1, v2, v1, v2, v3], axis=1)
+
+
+def below(v):
+    v1, v2, v3 = split(v, 3)
+    return jnp.concatenate([v1, v2, v1, v3, v2, v1], axis=0)
+
+
 def eliminate(a, first, last):
     rows = lax.broadcasted_iota(jnp.int32, (RANK, 1), 0)
     for k in range(first, last):
@@ -59,7 +68,7 @@
 
 
 def kernel(
-    x_hbm, g_hbm, f_hbm, q_hbm, upd_ref, qn_ref, m_ref, pt_ref, w_ref,
+    x_hbm, g_hbm, f_hbm, q_hbm, pm_ref, qn_ref, m_ref, pt_ref, w_ref,
     x_v, g_v, f_v, q_v, p_full,
     terms, core_recv, acc, plane_recv, z_group,
     m_peer, m_chip, st_v, s_send, s_recv, s_group, s_full,
@@ -199,7 +208,7 @@
             s = s + plane_recv[part, d, rows, :]
         z_group[part, z, rows, :] = s
         mine = z_group.at[part, z, rows]
-        for dz in range(1, 8):
+        for dz in (4, 3, 5, 2, 6, 1, 7):
             send(mine, mine, send_sem.at[2], z_sem.at[part], z_peer(dz))
 
     chip(0)
@@ -263,6 +272,17 @@
             send_sem.at[5], s_sem.at[0], plane_peer(dy, dx),
         )
 
+    take(s_recv.at[pl.ds(1, 15)], s_sem.at[0])
+    s = s_send[plane]
+    for d in range(1, 16):
+        s = s + s_recv[d]
+    s_group[core, z] = s
+    mine = s_group.at[core, z]
+    for dz in (4, 3, 5, 2, 6, 1, 7):
+        send(mine, mine, send_sem.at[6], s_sem.at[1], z_peer(dz))
+        send(mine, mine, send_sem.at[6], s_sem.at[1], z_peer(dz) + partner - me)
+    send(mine, mine, send_sem.at[6], s_sem.at[1], partner)
+    take(core_recv, send_sem.at[4])
     for part in range(PARTS):
         take(p_full.at[blocks(part), own], pair_sem.at[part])
     gram = jnp.zeros((3 * RANK, 3 * RANK), F32)
@@ -276,20 +296,8 @@
     cols = lax.broadcasted_iota(jnp.int32, (RANK, RANK), 1)
     eye = (rows == cols).astype(F32)
     a = jnp.concatenate([gram, eye], axis=1)
-    a = eliminate(a, 0, 8)
-
-    take(s_recv.at[pl.ds(1, 15)], s_sem.at[0])
-    s = s_send[plane]
-    for d in range(1, 16):
-        s = s + s_recv[d]
-    s_group[core, z] = s
-    mine = s_group.at[core, z]
-    for dz in (4, 3, 5, 2, 6, 1, 7):
-        send(mine, mine, send_sem.at[6], s_sem.at[1], z_peer(dz))
-        send(mine, mine, send_sem.at[6], s_sem.at[1], z_peer(dz) + partner - me)
-    send(mine, mine, send_sem.at[6], s_sem.at[1], partner)
-    take(core_recv, send_sem.at[4])
-    a = eliminate(a, 8, 36)
+    a = eliminate(a, 0, 24)
+
     take(s_recv.at[pl.ds(1, 15)], s_sem.at[1])
     s = s_group[:, 0]
     for k in range(1, 8):
@@ -299,10 +307,11 @@
     for dy, dx in PLANE:
         send(mine, mine, send_sem.at[7], s_sem.at[2], plane_peer(dy, dx))
     take(s_recv.at[pl.ds(1, 15)], send_sem.at[5])
-    a = eliminate(a, 36, 64)
+    a = eliminate(a, 24, 64)
     diag = jnp.sum(a[:, 0:64] * eye, axis=1, keepdims=True)
     inv = a[:, 64:128] * (1.0 / jnp.sqrt(diag))
-    inv_t = inv.T
+    left, left_t = beside(inv), beside(inv.T)
+    pm_ref[...] = pt_ref[pl.ds(pl.multiple_of(me * 16, 16), 16), :]
     take(s_full.at[pl.ds(1, 15)], s_sem.at[2])
 
     s = jnp.concatenate(
@@ -313,34 +322,34 @@
         ],
         axis=0,
     )
-    qn = jnp.dot(inv, s, precision=HIGH, preferred_element_type=F32) * (1.0 / N_DP)
-    w = jnp.dot(inv_t, qn, precision=HIGH, preferred_element_type=F32)
+    qn = nn(left, below(s)) * (1.0 / N_DP)
+    w = nn(left_t, below(qn))
     w1, w2 = split(w, 2)
     w = jnp.concatenate([w1, w1, w2, w2], axis=0)
     w_ref[...] = w
     qn_ref[...] = qn
-    p = pt_ref[pl.ds(pl.multiple_of(me * 16, 16), 16), :]
-    upd_ref[...] = nn(jnp.concatenate([p, p], axis=1), w)
     take(s_recv.at[pl.ds(1, 15)], send_sem.at[6])
     take(s_full.at[pl.ds(1, 15)], send_sem.at[7])
 
 
-def finish(upd_v, qn_v, m_v, pt_v, w_v, upd_hbm, qn_hbm, out_hbm, out_v, small_sem):
-    small = [
-        pltpu.make_async_copy(upd_v, upd_hbm, small_sem.at[0]),
-        pltpu.make_async_copy(qn_v, qn_hbm, small_sem.at[1]),
+def finish(pm_v, qn_v, m_v, pt_v, w_v, upd_hbm, qn_hbm, out_hbm, out_v, upd_v, sem):
+    copies = [
+        pltpu.make_async_copy(qn_v, qn_hbm, sem.at[0]),
+        pltpu.make_async_copy(upd_v, upd_hbm, sem.at[1]),
     ]
-    for copy in small:
-        copy.start()
+    copies[0].start()
     w = w_v[...]
     for i in range(D // CH):
         at = pl.ds(i * CH, CH)
         p = pt_v[at, :]
         out_v[at, :] = (m_v[at, :] - nn(jnp.concatenate([p, p], axis=1), w)).astype(BF16)
-        pltpu.make_async_copy(out_v.at[at, :], out_hbm.at[at, :], small_sem.at[2]).start()
-    for copy in small:
+        pltpu.make_async_copy(out_v.at[at, :], out_hbm.at[at, :], sem.at[2]).start()
+    p = pm_v[...]
+    upd_v[...] = nn(jnp.concatenate([p, p], axis=1), w)
+    copies[1].start()
+    for copy in copies:
         copy.wait()
-    pltpu.make_async_copy(out_v, out_hbm, small_sem.at[2]).wait()
+    pltpu.make_async_copy(out_v, out_hbm, sem.at[2]).wait()
 
 
 def body(inputs, out_grads, feedback, q_start):
@@ -348,10 +357,10 @@
     vmem = pltpu.VMEM
     in_vmem = pl.BlockSpec(memory_space=vmem)
     in_any = pl.BlockSpec(memory_space=pl.ANY)
-    upd, qn, m, pt, w = pl.pallas_call(
+    pm, qn, m, pt, w = pl.pallas_call(
         kernel,
         out_shape=(
-            vmem((D // N_DP, KV), F32),
+            vmem((D // N_DP, 128), BF16),
             vmem((RANK, KV), F32),
             vmem((D, KV), F32),
             vmem((D, 128), BF16),
@@ -393,9 +402,9 @@
         ),
         in_specs=[in_vmem] * 5,
         out_specs=(in_any,) * 3,
-        scratch_shapes=[vmem((D, KV), BF16), dma((3,))],
+        scratch_shapes=[vmem((D, KV), BF16), vmem((D // N_DP, KV), F32), dma((3,))],
         compiler_params=pltpu.CompilerParams(vmem_limit_bytes=16 * MIB),
-    )(upd, qn, m, pt, w)
+    )(pm, qn, m, pt, w)
     return upd, qn.T, new_feedback
 
 

time: 49.2 us -> 48.8 us (level)
  no operation moved by 1% of the time
where the time goes in v6:
time: 48.8 us; the launch traced here: 48.7 us
  Pallas kernels  48.1 us (99%)
  between operations  0.64 us (1%)
    pallas_call x1, Pallas kernels, body(): pl.pallas_call(kernel, out_shape=(vmem((D // N_DP, 128), BF16), vmem((RAN...  45.7 us
    pallas_call x1, Pallas kernels, body(): pl.pallas_call(finish, out_shape=(jax.ShapeDtypeStruct((D // N_DP, KV), F...  2.33 us

profile of v6, /device:TPU:1, one launch (start us, length us, event | category | flops | bytes accessed | tf_op | source)
XLA Modules:
  0.0 48.7 jit_solution(7490885990583641883)
XLA Ops:
  0.6 45.7 %shard_map.67 = (bf16[16,128]{1,0:T(8,128)(2,1)S(1)}, f32[64,512]{1,0:T(8,128)S(1)}, f32[4096,512]{1,0:T(8,128)S(1)}, bf16[4096,128]{1,0:T(8,128)(2,1)S(1)}, bf16[256,512]{1,0:T(8,128)(2,1)S(1)}) custom-call(bf16[256,4096]{1,0:T(8,128)(2,1)} %x_hbm.1, bf16[256,512]{1,0:T(8,128)(2,1)} %g_hbm.1, bf16[4096,512]{1,0:T(8,128)(2,1)} %f_hbm.1, f32[64,512]{1,0:T(8,128)} %bitcast.2), custom_call_target="tpu_custom_call" | custom-call | tf_op jit(solution)/shard_map/pallas_call | solution.py:360
  46.4 2.3 %shard_map.68 = (f32[16,512]{1,0:T(8,128)}, f32[64,512]{1,0:T(8,128)}, bf16[4096,512]{1,0:T(8,128)(2,1)}) custom-call(bf16[16,128]{1,0:T(8,128)(2,1)S(1)} %get-tuple-element.11.pm_v, f32[64,512]{1,0:T(8,128)S(1)} %get-tuple-element.12.qn_v, f32[4096,512]{1,0:T(8,128)S(1)} %get-tuple-element.13.m_v, bf16[4096,128]{1,0:T(8,128)(2,1)S(1)} %get-tuple-element.14.pt_v, ...), custom_call_target="tpu_custom_call" | custom-call | tf_op jit(solution)/shard_map/pallas_call | solution.py:396
